TPU v7x, 512 devices: a whole 4x8x8 slice. The times are simulated.
512 devices in a mesh: rep: 16 (over z, x_lo), fsdp: 32 (over x_hi, y, core).
Axes of the slice: x: 4 (x_hi: 2, x_lo: 2; x = x_hi * 2 + x_lo), y: 8, z: 8, core: 2. Of those that a mesh axis runs over, the one named last changes fastest.
Arguments:
- cotangent: bfloat16 [163840, 4096], P(('rep', 'fsdp')), may hold values from -6 to 6
- gate_pre: bfloat16 [163840, 256], P(('rep', 'fsdp')), may hold values from -6 to 6
- up_pre: bfloat16 [163840, 256], P(('rep', 'fsdp')), may hold values from -24 to 24
- slab_weight: bfloat16 [256, 4096], P('fsdp'), may hold values from -0.09375 to 0.09375
- base_params: float32 [256, 4096], P('fsdp'), may hold values from -6 to 6
- momentum: float32 [2, 256, 4096], P(None, 'fsdp'), may hold values from -4 to 4
- codes: int32 [16, 256, 4096], P('rep', 'fsdp'), may hold values from -8 to 7
- scales: float32 [16, 256, 32], P('rep', 'fsdp'), may hold values from 0.05 to 0.5
- frag_index: int32 [1], replicated, may hold values from 0 to 1
Outputs:
- inner_grad: float32 [16, 256, 4096], P('rep', 'fsdp')
- grad_gate: bfloat16 [163840, 256], P(('rep', 'fsdp'))
- grad_up: bfloat16 [163840, 256], P(('rep', 'fsdp'))
- new_params: float32 [256, 4096], P('fsdp')
- new_momentum: float32 [256, 4096], P('fsdp')
All inputs are finite; a program needn't handle non-finite values.
Results may differ from a plain program's by a relative error of at most 0.0029.
Values may be sent and summed in bfloat16 or wider, within the bound.
No kernel may reach another device: no remote copies, remote signals or barrier semaphores. Data moves between devices by JAX's collectives and lax.ppermute only.
A program may use at most 64 MiB of HBM per device.

v0:
```python
import math

import jax
import jax.numpy as jnp
from jax import lax
from jax.sharding import PartitionSpec as P


def outer_update(summed, replicas, old_momentum, base_rows):
    mean_delta = summed / replicas
    new_momentum = 0.9 * old_momentum + mean_delta
    new_params = base_rows - 0.7 * (mean_delta + 0.9 * new_momentum)
    return (new_params, new_momentum)


def per_device(
    cotangent, gate_pre, up_pre, slab_weight, base_params, momentum, codes, scales, frag_index
):
    gate = gate_pre.astype(jnp.float32)
    upper = up_pre.astype(jnp.float32)
    silu_gate = jax.nn.silu(gate)
    hidden = (silu_gate * upper).astype(jnp.bfloat16)
    frag_rows = codes.shape[1]
    width = codes.shape[2]
    blocks = (
        codes[0].astype(jnp.float32).reshape(frag_rows, width // 128, 128) * scales[0][..., None]
    )
    local_delta = blocks.reshape(frag_rows, width)
    old_momentum = lax.dynamic_index_in_dim(momentum, frag_index[0], 0, keepdims=False)
    replicas = lax.axis_size("rep")
    summed = lax.psum(local_delta, "rep")
    new_params, new_momentum = outer_update(summed, replicas, old_momentum, base_params)
    grad_hidden = jnp.einsum(
        "td,rd->tr",
        cotangent,
        lax.all_gather(slab_weight, "fsdp", axis=0, tiled=True),
        preferred_element_type=jnp.float32,
    )
    sigma = jax.nn.sigmoid(gate)
    grad_up = (grad_hidden * silu_gate).astype(jnp.bfloat16)
    grad_gate = (grad_hidden * upper * sigma * (1.0 + gate * (1.0 - sigma))).astype(jnp.bfloat16)
    grad_sum = lax.psum_scatter(
        lax.dot_general(
            hidden, cotangent, (((0,), (0,)), ((), ())), preferred_element_type=jnp.float32
        ),
        "fsdp",
        scatter_dimension=0,
        tiled=True,
    )
    factor = 1.0 / math.sqrt(cotangent.shape[0] * lax.axis_size("fsdp"))
    inner_grad = (grad_sum * factor)[None]
    return (inner_grad, grad_gate, grad_up, new_params, new_momentum)


def solution(mesh):
    placed = (
        P(("rep", "fsdp"), None),
        P(("rep", "fsdp"), None),
        P(("rep", "fsdp"), None),
        P("fsdp", None),
        P("fsdp", None),
        P(None, "fsdp", None),
        P("rep", "fsdp", None),
        P("rep", "fsdp", None),
        P(),
    )
    return jax.shard_map(
        per_device,
        mesh=mesh,
        in_specs=placed,
        out_specs=(
            P("rep", "fsdp", None),
            P(("rep", "fsdp"), None),
            P(("rep", "fsdp"), None),
            P("fsdp", None),
            P("fsdp", None),
        ),
        check_vma=False,
    )
```

profile of v0, /device:TPU:1, one launch (start us, length us, event | category | flops | bytes accessed | tf_op | source)
XLA Modules:
  0.0 246.9 jit_solution(9946188099470862567)
XLA Ops:
  8.0 0.0 copy-start
  8.0 0.0 all-reduce.2.cloned.1.call-start
  8.1 0.9 copy.14
  9.0 1.7 bitcast_multiply_fusion
  10.6 0.0 all-reduce.2.cloned.1.call-update
  10.7 0.0 all-gather.2.cloned.1.call-start
  10.7 0.5 all-gather.2.cloned.1.call-update
  11.2 0.0 reduce-scatter.2.cloned.1.call-start
  11.3 0.0 copy-done
  11.3 4.3 %fusion.8 = f32[256,4096]{1,0:T(8,128)} fusion(bf16[320,4096]{1,0:T(8,128)(2,1)S(1)} %copy-done, bf16[320,256]{1,0:T(8,128)(2,1)} %param.11, bf16[320,256]{1,0:T(8,128)(2,1)} %param.10), kind=kOutput, calls=%fused_computation.14 | convolution fusion | flops 671744000 | bytes 7143424 | tf_op jit(solution)/shard_map/dot_general | solution.py:43
  15.6 0.0 copy-start.3
  15.6 0.0 copy-start.4
  15.6 0.0 copy-start.1
  15.6 0.0 copy-start.2
  15.6 0.0 reduce-scatter.2.cloned.1.call-update
  16.3 135.7 %all-reduce.2.cloned.1.call-done = f32[8,4096]{1,0:T(8,128)} async-done(((f32[8,4096]{1,0:T(8,128)}), f32[8,4096]{1,0:T(8,128)}) %all-reduce.2.cloned.1.call-update) | async-done | bytes 131088 | tf_op jit(solution)/shard_map/psum | solution.py:31
  152.0 0.0 copy-done.3
  152.0 0.0 copy-done.4
  152.0 1.6 multiply_subtract_fusion
  153.6 0.0 copy-done.1
  153.6 0.0 copy-done.2
  153.6 3.2 %multiply_convert_fusion = (bf16[320,256]{1,0:T(8,128)(2,1)}, bf16[320,256]{1,0:T(8,128)(2,1)}) fusion(bf16[320,256]{1,0:T(8,128)(2,1)S(1)} %copy-done.2, bf16[320,256]{1,0:T(8,128)(2,1)S(1)} %copy-done.1, bf16[320,4096]{1,0:T(8,128)(2,1)S(1)} %copy-done, bf16[256,4096]{1,0:T(8,128)(2,1)} %all-gather.2.cloned.1.call-done), kind=kOutput, calls=%fused_computation.13 | convolution fusion | flops 672317440 | bytes 5373952 | tf_op jit(solution)/shard_map/td,rd->tr/dot_general | solution.py:33
  156.9 81.0 %reduce-scatter.2.cloned.1.call-done = f32[8,4096]{1,0:T(8,128)} async-done(((f32[256,4096]{1,0:T(8,128)}), f32[8,4096]{1,0:T(8,128)}) %reduce-scatter.2.cloned.1.call-update) | async-done | bytes 131088 | tf_op jit(solution)/shard_map/reduce_scatter | solution.py:42
  237.9 1.6 multiply_bitcast_fusion
  (1 shorter events, 0.0 us)
Async XLA Ops:
  8.0 3.3 %copy-start = (bf16[320,4096]{1,0:T(8,128)(2,1)S(1)}, bf16[320,4096]{1,0:T(8,128)(2,1)}, u32[]{:S(2)}) copy-start(bf16[320,4096]{1,0:T(8,128)(2,1)} %param.9) | copy-start | bytes 7864324
  8.0 144.0 %all-reduce.2.cloned.1.call-start = ((), (), s32[]{:S(2)}) async-start(), calls=%async_computation.3 | async-start | bytes 262144 | tf_op jit(solution)/shard_map/psum | solution.py:31
  10.7 143.0 %all-gather.2.cloned.1.call-start = ((), (), s32[]{:S(2)}) async-start(), calls=%async_computation.2 | async-start | bytes 2162688 | tf_op jit(solution)/shard_map/all_gather | solution.py:36
  11.2 226.6 %reduce-scatter.2.cloned.1.call-start = ((), (), s32[]{:S(2)}) async-start(), calls=%async_computation.1 | async-start | bytes 4325376 | tf_op jit(solution)/shard_map/reduce_scatter | solution.py:42
  15.6 136.4 %copy-start.3 = (f32[8,4096]{1,0:T(8,128)S(1)}, f32[8,4096]{1,0:T(8,128)}, u32[]{:S(2)}) copy-start(f32[8,4096]{1,0:T(8,128)} %param.13) | copy-start | bytes 393220
  15.6 136.4 %copy-start.4 = (f32[2,8,4096]{2,1,0:T(8,128)S(1)}, f32[2,8,4096]{2,1,0:T(8,128)}, u32[]{:S(2)}) copy-start(f32[2,8,4096]{2,1,0:T(8,128)} %param.14) | copy-start | bytes 786436
  15.6 138.1 %copy-start.1 = (bf16[320,256]{1,0:T(8,128)(2,1)S(1)}, bf16[320,256]{1,0:T(8,128)(2,1)}, u32[]{:S(2)}) copy-start(bf16[320,256]{1,0:T(8,128)(2,1)} %param.11) | copy-start | bytes 491524
  15.6 138.1 %copy-start.2 = (bf16[320,256]{1,0:T(8,128)(2,1)S(1)}, bf16[320,256]{1,0:T(8,128)(2,1)}, u32[]{:S(2)}) copy-start(bf16[320,256]{1,0:T(8,128)(2,1)} %param.10) | copy-start | bytes 491524
Sparse Core Ops, SparseCore 0:
  12.6 139.3 all-reduce.1
Sparse Core Ops, SparseCore 1:
  14.5 91.3 all-gather.1
  110.5 127.3 reduce-scatter.1
where the time goes:
time: 251 us; the launch traced here: 247 us
  waiting for transfers between devices  217 us (86%)
  between operations  16.2 us (6%)
  matrix products  7.48 us (3%)
  other arithmetic  4.87 us (2%)
    psum x1, waiting for transfers between devices, per_device(): summed = lax.psum(local_delta, 'rep')  136 us
    reduce_scatter x1, waiting for transfers between devices, per_device(): lax.psum_scatter(lax.dot_general(hidden, cotangent, (((0,), (0,)), ((), (...  81 us
  transfers between devices with their start and end apart: 3, of which 2 were waited for; matrix products, arithmetic and copies ran while one was open for 4% of the time, Pallas kernels for 0%

commit v1 on v0

v1 whole, which is shorter than its diff:
```python
import math

import jax
import jax.numpy as jnp
from jax import lax
from jax.sharding import Mesh, PartitionSpec as P

REP = ("z", "xl")
FSDP = ("xh", "y", "core")
OFFSETS = (-3, 0, 3, -2, 1, 4, -1, 2)


def shift(value, axis, step):
    n = lax.axis_size(axis)
    return lax.ppermute(value, axis, [(i, (i + step) % n) for i in range(n)])


def swap(value, axis, bit=1):
    n = lax.axis_size(axis)
    return lax.ppermute(value, axis, [(i, i ^ bit) for i in range(n)])


def chunk_owner(core_rel, y_offset, x_rel):
    x = lax.axis_index("xh") ^ x_rel
    y = (lax.axis_index("y") + y_offset) % 8
    core = lax.axis_index("core") ^ core_rel
    return (x * 8 + y) * 2 + core


def selector(order):
    owners = jnp.stack([chunk_owner(*place) for place in order])
    rows = (owners[:, None] * 8 + jnp.arange(8)[None, :]).reshape(256, 1)
    return (rows == jnp.arange(256)[None, :]).astype(jnp.bfloat16)


def outer_update(summed, replicas, old_momentum, base_rows):
    mean_delta = summed / replicas
    new_momentum = 0.9 * old_momentum + mean_delta
    new_params = base_rows - 0.7 * (mean_delta + 0.9 * new_momentum)
    return (new_params, new_momentum)


def gather_rows(w):
    w = jnp.concatenate([w, swap(w, "xh")])
    up, down = shift(w, "y", 3), shift(w, "y", -3)
    own = jnp.concatenate([up, w, down])
    from_above = shift(own, "y", -1)
    from_below = shift(own[16:], "y", 1)
    half = jnp.concatenate([own, from_above, from_below])
    return jnp.concatenate([half, swap(half, "core")])


def reduce_rows(part):
    bf16 = jnp.bfloat16
    s = part[:128] + swap(part[128:].astype(bf16), "core").astype(jnp.float32)
    s = s[:64] + swap(s[64:].astype(bf16), "xh").astype(jnp.float32)
    to_up, to_down = s[24:48].astype(bf16), s[48:].astype(bf16)
    below, above = shift(to_up, "y", 1), shift(to_down, "y", -1)
    t = s[:24] + below.astype(jnp.float32)
    t = jnp.concatenate([t[:8], t[8:] + above.astype(jnp.float32)])
    far_up = shift(t[16:].astype(bf16), "y", 3)
    far_down = shift(t[:8].astype(bf16), "y", -3)
    return t[8:16] + far_up.astype(jnp.float32) + far_down.astype(jnp.float32)


def sum_replicas(delta):
    s = delta + swap(delta, "xl")
    for bit in (1, 2, 4):
        s = s + swap(s, "z", bit)
    return s


def per_device(
    cotangent, gate_pre, up_pre, slab_weight, base_params, momentum, codes, scales, frag_index
):
    gate = gate_pre.astype(jnp.float32)
    upper = up_pre.astype(jnp.float32)
    silu_gate = jax.nn.silu(gate)
    hidden = (silu_gate * upper).astype(jnp.bfloat16)
    frag_rows = codes.shape[1]
    width = codes.shape[2]
    blocks = (
        codes[0].astype(jnp.float32).reshape(frag_rows, width // 128, 128) * scales[0][..., None]
    )
    local_delta = blocks.reshape(frag_rows, width)
    old_momentum = lax.dynamic_index_in_dim(momentum, frag_index[0], 0, keepdims=False)
    summed = sum_replicas(local_delta)
    new_params, new_momentum = outer_update(summed, 16, old_momentum, base_params)

    pick = selector([(c, o, x) for c in (0, 1) for x in (0, 1) for o in OFFSETS])
    hidden_rel = jnp.dot(hidden, pick.T)
    part = lax.dot_general(
        hidden_rel, cotangent, (((0,), (0,)), ((), ())), preferred_element_type=jnp.float32
    )
    factor = 1.0 / math.sqrt(10240)
    inner_grad = (reduce_rows(part) * factor)[None]

    place = selector([(c, o, x) for c in (0, 1) for o in OFFSETS for x in (0, 1)])
    weight = jnp.dot(place.T, gather_rows(slab_weight))
    grad_hidden = jnp.einsum("td,rd->tr", cotangent, weight, preferred_element_type=jnp.float32)
    sigma = jax.nn.sigmoid(gate)
    grad_up = (grad_hidden * silu_gate).astype(jnp.bfloat16)
    grad_gate = (grad_hidden * upper * sigma * (1.0 + gate * (1.0 - sigma))).astype(jnp.bfloat16)
    return (inner_grad, grad_gate, grad_up, new_params, new_momentum)


def solution(mesh):
    fine = Mesh(mesh.devices.reshape(8, 2, 2, 8, 2), REP + FSDP)
    tokens = P(REP + FSDP, None)
    return jax.shard_map(
        per_device,
        mesh=fine,
        in_specs=(
            tokens,
            tokens,
            tokens,
            P(FSDP, None),
            P(FSDP, None),
            P(None, FSDP, None),
            P(REP, FSDP, None),
            P(REP, FSDP, None),
            P(),
        ),
        out_specs=(P(REP, FSDP, None), tokens, tokens, P(FSDP, None), P(FSDP, None)),
        check_vma=False,
    )
```

time: 251 us -> 114 us (0.45)
  waiting for transfers between devices: 217 us -> 21.1 us
  starting transfers between devices: 0.12 us -> 72.4 us
  between operations: 16.2 us -> 1.96 us
  local copies, waits for them, and re-layouts: 0.94 us -> 4.94 us
    psum x1 -> x0, waiting for transfers between devices: 136 us -> none  [per_device(): summed = lax.psum(local_delta, 'rep')]
    reduce_scatter x1 -> x0, waiting for transfers between devices: 81 us -> none  [per_device(): lax.psum_scatter(lax.dot_general(hidden, cotangent, (((0,), (0,)), ((), (...]
    ppermute x0 -> x16, starting transfers between devices: none -> 72.4 us  [the longest x8 44.9 us: swap(): return lax.ppermute(value, axis, [(i, i ^ bit) for i in range(n)])]
    ppermute x0 -> x16, waiting for transfers between devices: none -> 21.1 us  [the longest x8 17.5 us: swap(): return lax.ppermute(value, axis, [(i, i ^ bit) for i in range(n)])]
    slice x0 -> x6, local copies, waits for them, and re-layouts: none -> 2.85 us  [the longest x1 2.75 us: reduce_rows(): s = part[:128] + swap(part[128:].astype(bf16), 'core').astype(jnp.float32)]
  transfers between devices with their start and end apart: 3 -> 16, of which waited for: 2 -> 5; matrix products, arithmetic and copies ran while one was open for 4% -> 6% of each run, Pallas kernels for 0% -> 0%
where the time goes in v1:
time: 114 us; the launch traced here: 112 us
  starting transfers between devices  72.4 us (64%)
  waiting for transfers between devices  21.1 us (19%)
  matrix products  8.48 us (7%)
  local copies, waits for them, and re-layouts  4.94 us (4%)
  other arithmetic  3.46 us (3%)
  between operations  1.96 us (2%)
    ppermute x8, starting transfers between devices, swap(): return lax.ppermute(value, axis, [(i, i ^ bit) for i in range(n)])  44.9 us
    ppermute x8, starting transfers between devices, shift(): return lax.ppermute(value, axis, [(i, (i + step) % n) for i in range(n)])  27.5 us
    ppermute x8, waiting for transfers between devices, swap(): return lax.ppermute(value, axis, [(i, i ^ bit) for i in range(n)])  17.5 us
    dot_general x1, matrix products, per_device(): lax.dot_general(hidden_rel, cotangent, (((0,), (0,)), ((), ())), preferre...  4.63 us
    dot_general x1, matrix products, per_device(): jnp.einsum('td,rd->tr', cotangent, weight, preferred_element_type=jnp.flo...  3.85 us
    ppermute x8, waiting for transfers between devices, shift(): return lax.ppermute(value, axis, [(i, (i + step) % n) for i in range(n)])  3.57 us
    slice x1, local copies, waits for them, and re-layouts, reduce_rows(): s = part[:128] + swap(part[128:].astype(bf16), 'core').astype(jnp.float32)  2.75 us
  transfers between devices with their start and end apart: 16, of which 5 were waited for; matrix products, arithmetic and copies ran while one was open for 6% of the time, Pallas kernels for 0%

profile of v1, /device:TPU:1, one launch (start us, length us, event | category | flops | bytes accessed | tf_op | source)
XLA Modules:
  0.0 112.3 jit_solution(17313518290842786588)
XLA Ops:
  2.4 4.6 %fusion.6 = f32[256,4096]{1,0:T(8,128)} fusion(bf16[320,4096]{1,0:T(8,128)(2,1)S(1)} %copy-done, bf16[320,256]{1,0:T(8,128)(2,1)} %param.11, bf16[320,256]{1,0:T(8,128)(2,1)} %param.10, s32[256]{0:T(256)S(1)} %add.530), kind=kOutput, calls=%fused_computation.5 | convolution fusion | flops 713752576 | bytes 7144448 | tf_op jit(solution)/shard_map/dot_general | solution.py:92
  7.0 2.8 %slice.78 = bf16[128,4096]{1,0:T(8,128)(2,1)} slice(f32[256,4096]{1,0:T(8,128)} %fusion.6), slice={[128:256], [0:4096]} | slice | bytes 2097152 | tf_op jit(solution)/shard_map/slice | solution.py:55
  9.8 8.8 %collective-permute-start = (bf16[128,4096]{1,0:T(8,128)(2,1)}, bf16[128,4096]{1,0:T(8,128)(2,1)}, u32[]{:S(2)}, u32[]{:S(2)}) collective-permute-start(bf16[128,4096]{1,0:T(8,128)(2,1)} %slice.78), channel_id=1, source_target_pairs={{0,1},{1,0},{2,3},{3,2},{4,5},{5,4},{6,7},{7,6},{8,9},{9,8},{10,11... | collective-permute-start | bytes 3145736 | tf_op jit(solution)/shard_map/ppermute | solution.py:20
  18.6 1.9 %collective-permute-start.6 = (bf16[8,4096]{1,0:T(8,128)(2,1)S(1)}, bf16[8,4096]{1,0:T(8,128)(2,1)S(1)}, u32[]{:S(2)}, u32[]{:S(2)}) collective-permute-start(bf16[8,4096]{1,0:T(8,128)(2,1)S(1)} %copy-done.2), channel_id=1, source_target_pairs={{0,16},{16,0},{1,17},{17,1},{2,18},{18,2},{3,19},{19,3},{4,20},{20... | collective-permute-start | bytes 196616 | tf_op jit(solution)/shard_map/ppermute | solution.py:20
  20.7 1.9 %collective-permute-start.12 = (f32[8,4096]{1,0:T(8,128)S(1)}, f32[8,4096]{1,0:T(8,128)S(1)}, u32[]{:S(2)}, u32[]{:S(2)}) collective-permute-start(f32[8,4096]{1,0:T(8,128)S(1)} %bitcast_multiply_fusion), channel_id=1, source_target_pairs={{0,32},{32,0},{1,33},{33,1},{2,34},{34,2},{3,35},{35,3},{4,36},{36... | collective-permute-start | bytes 393224 | tf_op jit(solution)/shard_map/ppermute | solution.py:20
  22.8 2.9 %collective-permute-done.6 = bf16[8,4096]{1,0:T(8,128)(2,1)S(1)} collective-permute-done((bf16[8,4096]{1,0:T(8,128)(2,1)S(1)}, bf16[8,4096]{1,0:T(8,128)(2,1)S(1)}, u32[]{:S(2)}, u32[]{:S(2)}) %collective-permute-start.6) | collective-permute-done | bytes 65568 | tf_op jit(solution)/shard_map/ppermute | solution.py:20
  25.7 1.9 %collective-permute-start.7 = (bf16[16,4096]{1,0:T(8,128)(2,1)S(1)}, bf16[16,4096]{1,0:T(8,128)(2,1)S(1)}, u32[]{:S(2)}, u32[]{:S(2)}) collective-permute-start(bf16[16,4096]{1,0:T(8,128)(2,1)S(1)} %constant_dynamic-update-slice_fusion), channel_id=1, source_target_pairs={{0,6},{2,8},{4,10},{6,12},{8,14},{10,0},{12,2},{14,4},{1,7},{3,9},... | collective-permute-start | bytes 393224 | tf_op jit(solution)/shard_map/ppermute | solution.py:15
  27.6 6.4 %collective-permute-start.8 = (bf16[16,4096]{1,0:T(8,128)(2,1)S(1)}, bf16[16,4096]{1,0:T(8,128)(2,1)S(1)}, u32[]{:S(2)}, u32[]{:S(2)}) collective-permute-start(bf16[16,4096]{1,0:T(8,128)(2,1)S(1)} %constant_dynamic-update-slice_fusion), channel_id=1, source_target_pairs={{0,10},{2,12},{4,14},{6,0},{8,2},{10,4},{12,6},{14,8},{1,11},{3,13... | collective-permute-start | bytes 393224 | tf_op jit(solution)/shard_map/ppermute | solution.py:15
  34.8 1.9 %collective-permute-start.13 = (f32[8,4096]{1,0:T(8,128)S(1)}, f32[8,4096]{1,0:T(8,128)S(1)}, u32[]{:S(2)}, u32[]{:S(2)}) collective-permute-start(f32[8,4096]{1,0:T(8,128)S(1)} %add.542), channel_id=1, source_target_pairs={{0,64},{64,0},{128,192},{192,128},{256,320},{320,256},{384,448},{4... | collective-permute-start | bytes 393224 | tf_op jit(solution)/shard_map/ppermute | solution.py:20
  38.2 1.9 %collective-permute-start.9 = (bf16[48,4096]{1,0:T(8,128)(2,1)S(1)}, bf16[48,4096]{1,0:T(8,128)(2,1)S(1)}, u32[]{:S(2)}, u32[]{:S(2)}) collective-permute-start(bf16[48,4096]{1,0:T(8,128)(2,1)S(1)} %pad_maximum_fusion), channel_id=1, source_target_pairs={{0,14},{2,0},{4,2},{6,4},{8,6},{10,8},{12,10},{14,12},{1,15},{3,1}... | collective-permute-start | bytes 1179656 | tf_op jit(solution)/shard_map/ppermute | solution.py:15
  40.2 3.6 %collective-permute-start.10 = (bf16[32,4096]{1,0:T(8,128)(2,1)S(1)}, bf16[32,4096]{1,0:T(8,128)(2,1)S(1)}, u32[]{:S(2)}, u32[]{:S(2)}) collective-permute-start(bf16[32,4096]{1,0:T(8,128)(2,1)S(1)} %pad_maximum_fusion.1), channel_id=1, source_target_pairs={{0,2},{2,4},{4,6},{6,8},{8,10},{10,12},{12,14},{14,0},{1,3},{3,5},... | collective-permute-start | bytes 786440 | tf_op jit(solution)/shard_map/ppermute | solution.py:15
  43.9 10.1 %collective-permute-start.14 = (f32[8,4096]{1,0:T(8,128)S(1)}, f32[8,4096]{1,0:T(8,128)S(1)}, u32[]{:S(2)}, u32[]{:S(2)}) collective-permute-start(f32[8,4096]{1,0:T(8,128)S(1)} %add.543), channel_id=1, source_target_pairs={{0,128},{64,192},{128,0},{192,64},{256,384},{320,448},{384,256},{4... | collective-permute-start | bytes 393224 | tf_op jit(solution)/shard_map/ppermute | solution.py:20
  54.1 2.9 %collective-permute-done.14 = f32[8,4096]{1,0:T(8,128)S(1)} collective-permute-done((f32[8,4096]{1,0:T(8,128)S(1)}, f32[8,4096]{1,0:T(8,128)S(1)}, u32[]{:S(2)}, u32[]{:S(2)}) %collective-permute-start.14) | collective-permute-done | bytes 131104 | tf_op jit(solution)/shard_map/ppermute | solution.py:20
  57.1 11.9 %collective-permute-start.15 = (f32[8,4096]{1,0:T(8,128)S(1)}, f32[8,4096]{1,0:T(8,128)S(1)}, u32[]{:S(2)}, u32[]{:S(2)}) collective-permute-start(f32[8,4096]{1,0:T(8,128)S(1)} %add.544), channel_id=1, source_target_pairs={{0,256},{64,320},{128,384},{192,448},{256,0},{320,64},{384,128},{4... | collective-permute-start | bytes 393224 | tf_op jit(solution)/shard_map/ppermute | solution.py:20
  69.2 3.8 %collective-permute-start.11 = (bf16[128,4096]{1,0:T(8,128)(2,1)S(1)}, bf16[128,4096]{1,0:T(8,128)(2,1)S(1)}, u32[]{:S(2)}, u32[]{:S(2)}) collective-permute-start(bf16[128,4096]{1,0:T(8,128)(2,1)S(1)} %get-tuple-element.13), channel_id=1, source_target_pairs={{0,1},{1,0},{2,3},{3,2},{4,5},{5,4},{6,7},{7,6},{8,9},{9,8},{10,11... | collective-permute-start | bytes 3145736 | tf_op jit(solution)/shard_map/ppermute | solution.py:20
  73.0 1.5 %slice_add_fusion = f32[128,4096]{1,0:T(8,128)S(1)} fusion(f32[256,4096]{1,0:T(8,128)S(1)} %copy-done.1, bf16[128,4096]{1,0:T(8,128)(2,1)} %collective-permute-done), kind=kLoop, calls=%fused_computation.1 | loop fusion | flops 1048576 | bytes 5242880 | tf_op jit(solution)/shard_map/add | solution.py:55
  74.5 4.5 %collective-permute-start.1 = (bf16[64,4096]{1,0:T(8,128)(2,1)S(1)}, bf16[64,4096]{1,0:T(8,128)(2,1)S(1)}, u32[]{:S(2)}, u32[]{:S(2)}) collective-permute-start(bf16[64,4096]{1,0:T(8,128)(2,1)S(1)} %slice.79), channel_id=1, source_target_pairs={{0,16},{16,0},{1,17},{17,1},{2,18},{18,2},{3,19},{19,3},{4,20},{20... | collective-permute-start | bytes 1572872 | tf_op jit(solution)/shard_map/ppermute | solution.py:20
  79.8 11.6 %collective-permute-done.1 = bf16[64,4096]{1,0:T(8,128)(2,1)S(1)} collective-permute-done((bf16[64,4096]{1,0:T(8,128)(2,1)S(1)}, bf16[64,4096]{1,0:T(8,128)(2,1)S(1)}, u32[]{:S(2)}, u32[]{:S(2)}) %collective-permute-start.1) | collective-permute-done | bytes 524320 | tf_op jit(solution)/shard_map/ppermute | solution.py:20
  91.7 3.5 %collective-permute-start.2 = (bf16[24,4096]{1,0:T(8,128)(2,1)S(1)}, bf16[24,4096]{1,0:T(8,128)(2,1)S(1)}, u32[]{:S(2)}, u32[]{:S(2)}) collective-permute-start(bf16[24,4096]{1,0:T(8,128)(2,1)S(1)} %slice.57), channel_id=1, source_target_pairs={{0,2},{2,4},{4,6},{6,8},{8,10},{10,12},{12,14},{14,0},{1,3},{3,5},... | collective-permute-start | bytes 589832 | tf_op jit(solution)/shard_map/ppermute | solution.py:15
  95.2 3.1 %collective-permute-start.3 = (bf16[16,4096]{1,0:T(8,128)(2,1)S(1)}, bf16[16,4096]{1,0:T(8,128)(2,1)S(1)}, u32[]{:S(2)}, u32[]{:S(2)}) collective-permute-start(bf16[16,4096]{1,0:T(8,128)(2,1)S(1)} %slice.59), channel_id=1, source_target_pairs={{0,14},{2,0},{4,2},{6,4},{8,6},{10,8},{12,10},{14,12},{1,15},{3,1}... | collective-permute-start | bytes 393224 | tf_op jit(solution)/shard_map/ppermute | solution.py:15
  98.4 2.1 %collective-permute-done.2 = bf16[24,4096]{1,0:T(8,128)(2,1)S(1)} collective-permute-done((bf16[24,4096]{1,0:T(8,128)(2,1)S(1)}, bf16[24,4096]{1,0:T(8,128)(2,1)S(1)}, u32[]{:S(2)}, u32[]{:S(2)}) %collective-permute-start.2) | collective-permute-done | bytes 196640 | tf_op jit(solution)/shard_map/ppermute | solution.py:15
  100.6 1.9 %collective-permute-start.5 = (bf16[8,4096]{1,0:T(8,128)(2,1)S(1)}, bf16[8,4096]{1,0:T(8,128)(2,1)S(1)}, u32[]{:S(2)}, u32[]{:S(2)}) collective-permute-start(bf16[8,4096]{1,0:T(8,128)(2,1)S(1)} %slice.80), channel_id=1, source_target_pairs={{0,10},{2,12},{4,14},{6,0},{8,2},{10,4},{12,6},{14,8},{1,11},{3,13... | collective-permute-start | bytes 196616 | tf_op jit(solution)/shard_map/ppermute | solution.py:15
  102.6 5.2 %collective-permute-start.4 = (bf16[8,4096]{1,0:T(8,128)(2,1)S(1)}, bf16[8,4096]{1,0:T(8,128)(2,1)S(1)}, u32[]{:S(2)}, u32[]{:S(2)}) collective-permute-start(bf16[8,4096]{1,0:T(8,128)(2,1)S(1)} %slice.81), channel_id=1, source_target_pairs={{0,6},{2,8},{4,10},{6,12},{8,14},{10,0},{12,2},{14,4},{1,7},{3,9},... | collective-permute-start | bytes 196616 | tf_op jit(solution)/shard_map/ppermute | solution.py:15
  107.8 3.8 %multiply_convert_fusion = (bf16[320,256]{1,0:T(8,128)(2,1)}, bf16[320,256]{1,0:T(8,128)(2,1)}) fusion(bf16[320,256]{1,0:T(8,128)(2,1)S(1)} %copy-done.4, bf16[320,256]{1,0:T(8,128)(2,1)S(1)} %copy-done.3, bf16[320,4096]{1,0:T(8,128)(2,1)S(1)} %copy-done, bf16[256,4096]{1,0:T(8,128)(2,1)} %copy-done.8, s32[256]{0:T(256)S(1)} %add.540), kind=kOutput, calls=%fused_computation.24 | convolution fusion | flops 1209253888 | bytes 5374976 | tf_op jit(solution)/shard_map/td,rd->tr/dot_general | solution.py:100
  (66 shorter events, 5.6 us)
Async XLA Ops:
  2.4 16.2 %copy-start.2 = (bf16[8,4096]{1,0:T(8,128)(2,1)S(1)}, bf16[8,4096]{1,0:T(8,128)(2,1)}, u32[]{:S(2)}) copy-start(bf16[8,4096]{1,0:T(8,128)(2,1)} %param.12) | copy-start | bytes 196612
  7.0 13.5 %copy-start.9 = (f32[1,8,32]{2,1,0:T(8,128)S(1)}, f32[1,8,32]{2,1,0:T(8,128)}, u32[]{:S(2)}) copy-start(f32[1,8,32]{2,1,0:T(8,128)} %param.16) | copy-start | bytes 3076
  7.0 13.6 %copy-start.5 = (s32[1,8,4096]{2,1,0:T(8,128)S(1)}, s32[1,8,4096]{2,1,0:T(8,128)}, u32[]{:S(2)}) copy-start(s32[1,8,4096]{2,1,0:T(8,128)} %param.15) | copy-start | bytes 393220
  9.8 63.2 %collective-permute-start = (bf16[128,4096]{1,0:T(8,128)(2,1)}, bf16[128,4096]{1,0:T(8,128)(2,1)}, u32[]{:S(2)}, u32[]{:S(2)}) collective-permute-start(bf16[128,4096]{1,0:T(8,128)(2,1)} %slice.78), channel_id=1, source_target_pairs={{0,1},{1,0},{2,3},{3,2},{4,5},{5,4},{6,7},{7,6},{8,9},{9,8},{10,11... | collective-permute-start | bytes 3145736 | tf_op jit(solution)/shard_map/ppermute | solution.py:20
  18.6 7.1 %collective-permute-start.6 = (bf16[8,4096]{1,0:T(8,128)(2,1)S(1)}, bf16[8,4096]{1,0:T(8,128)(2,1)S(1)}, u32[]{:S(2)}, u32[]{:S(2)}) collective-permute-start(bf16[8,4096]{1,0:T(8,128)(2,1)S(1)} %copy-done.2), channel_id=1, source_target_pairs={{0,16},{16,0},{1,17},{17,1},{2,18},{18,2},{3,19},{19,3},{4,20},{20... | collective-permute-start | bytes 196616 | tf_op jit(solution)/shard_map/ppermute | solution.py:20
  20.7 14.1 %collective-permute-start.12 = (f32[8,4096]{1,0:T(8,128)S(1)}, f32[8,4096]{1,0:T(8,128)S(1)}, u32[]{:S(2)}, u32[]{:S(2)}) collective-permute-start(f32[8,4096]{1,0:T(8,128)S(1)} %bitcast_multiply_fusion), channel_id=1, source_target_pairs={{0,32},{32,0},{1,33},{33,1},{2,34},{34,2},{3,35},{35,3},{4,36},{36... | collective-permute-start | bytes 393224 | tf_op jit(solution)/shard_map/ppermute | solution.py:20
  25.7 11.1 %collective-permute-start.7 = (bf16[16,4096]{1,0:T(8,128)(2,1)S(1)}, bf16[16,4096]{1,0:T(8,128)(2,1)S(1)}, u32[]{:S(2)}, u32[]{:S(2)}) collective-permute-start(bf16[16,4096]{1,0:T(8,128)(2,1)S(1)} %constant_dynamic-update-slice_fusion), channel_id=1, source_target_pairs={{0,6},{2,8},{4,10},{6,12},{8,14},{10,0},{12,2},{14,4},{1,7},{3,9},... | collective-permute-start | bytes 393224 | tf_op jit(solution)/shard_map/ppermute | solution.py:15
  27.6 10.6 %collective-permute-start.8 = (bf16[16,4096]{1,0:T(8,128)(2,1)S(1)}, bf16[16,4096]{1,0:T(8,128)(2,1)S(1)}, u32[]{:S(2)}, u32[]{:S(2)}) collective-permute-start(bf16[16,4096]{1,0:T(8,128)(2,1)S(1)} %constant_dynamic-update-slice_fusion), channel_id=1, source_target_pairs={{0,10},{2,12},{4,14},{6,0},{8,2},{10,4},{12,6},{14,8},{1,11},{3,13... | collective-permute-start | bytes 393224 | tf_op jit(solution)/shard_map/ppermute | solution.py:15
  34.8 9.1 %collective-permute-start.13 = (f32[8,4096]{1,0:T(8,128)S(1)}, f32[8,4096]{1,0:T(8,128)S(1)}, u32[]{:S(2)}, u32[]{:S(2)}) collective-permute-start(f32[8,4096]{1,0:T(8,128)S(1)} %add.542), channel_id=1, source_target_pairs={{0,64},{64,0},{128,192},{192,128},{256,320},{320,256},{384,448},{4... | collective-permute-start | bytes 393224 | tf_op jit(solution)/shard_map/ppermute | solution.py:20
  38.2 30.8 %collective-permute-start.9 = (bf16[48,4096]{1,0:T(8,128)(2,1)S(1)}, bf16[48,4096]{1,0:T(8,128)(2,1)S(1)}, u32[]{:S(2)}, u32[]{:S(2)}) collective-permute-start(bf16[48,4096]{1,0:T(8,128)(2,1)S(1)} %pad_maximum_fusion), channel_id=1, source_target_pairs={{0,14},{2,0},{4,2},{6,4},{8,6},{10,8},{12,10},{14,12},{1,15},{3,1}... | collective-permute-start | bytes 1179656 | tf_op jit(solution)/shard_map/ppermute | solution.py:15
  40.2 32.8 %copy-start.1 = (f32[256,4096]{1,0:T(8,128)S(1)}, f32[256,4096]{1,0:T(8,128)}, u32[]{:S(2)}) copy-start(f32[256,4096]{1,0:T(8,128)} %fusion.6) | copy-start | bytes 12582916
  40.2 28.9 %collective-permute-start.10 = (bf16[32,4096]{1,0:T(8,128)(2,1)S(1)}, bf16[32,4096]{1,0:T(8,128)(2,1)S(1)}, u32[]{:S(2)}, u32[]{:S(2)}) collective-permute-start(bf16[32,4096]{1,0:T(8,128)(2,1)S(1)} %pad_maximum_fusion.1), channel_id=1, source_target_pairs={{0,2},{2,4},{4,6},{6,8},{8,10},{10,12},{12,14},{14,0},{1,3},{3,5},... | collective-permute-start | bytes 786440 | tf_op jit(solution)/shard_map/ppermute | solution.py:15
  43.9 13.1 %collective-permute-start.14 = (f32[8,4096]{1,0:T(8,128)S(1)}, f32[8,4096]{1,0:T(8,128)S(1)}, u32[]{:S(2)}, u32[]{:S(2)}) collective-permute-start(f32[8,4096]{1,0:T(8,128)S(1)} %add.543), channel_id=1, source_target_pairs={{0,128},{64,192},{128,0},{192,64},{256,384},{320,448},{384,256},{4... | collective-permute-start | bytes 393224 | tf_op jit(solution)/shard_map/ppermute | solution.py:20
  57.1 22.0 %collective-permute-start.15 = (f32[8,4096]{1,0:T(8,128)S(1)}, f32[8,4096]{1,0:T(8,128)S(1)}, u32[]{:S(2)}, u32[]{:S(2)}) collective-permute-start(f32[8,4096]{1,0:T(8,128)S(1)} %add.544), channel_id=1, source_target_pairs={{0,256},{64,320},{128,384},{192,448},{256,0},{320,64},{384,128},{4... | collective-permute-start | bytes 393224 | tf_op jit(solution)/shard_map/ppermute | solution.py:20
  69.1 9.9 %copy-start.6 = (f32[8,4096]{1,0:T(8,128)S(1)}, f32[8,4096]{1,0:T(8,128)}, u32[]{:S(2)}) copy-start(f32[8,4096]{1,0:T(8,128)} %param.13) | copy-start | bytes 393220
  69.2 9.9 %copy-start.7 = (f32[2,8,4096]{2,1,0:T(8,128)S(1)}, f32[2,8,4096]{2,1,0:T(8,128)}, u32[]{:S(2)}) copy-start(f32[2,8,4096]{2,1,0:T(8,128)} %param.14) | copy-start | bytes 786436
  69.2 29.1 %collective-permute-start.11 = (bf16[128,4096]{1,0:T(8,128)(2,1)S(1)}, bf16[128,4096]{1,0:T(8,128)(2,1)S(1)}, u32[]{:S(2)}, u32[]{:S(2)}) collective-permute-start(bf16[128,4096]{1,0:T(8,128)(2,1)S(1)} %get-tuple-element.13), channel_id=1, source_target_pairs={{0,1},{1,0},{2,3},{3,2},{4,5},{5,4},{6,7},{7,6},{8,9},{9,8},{10,11... | collective-permute-start | bytes 3145736 | tf_op jit(solution)/shard_map/ppermute | solution.py:20
  74.5 16.9 %collective-permute-start.1 = (bf16[64,4096]{1,0:T(8,128)(2,1)S(1)}, bf16[64,4096]{1,0:T(8,128)(2,1)S(1)}, u32[]{:S(2)}, u32[]{:S(2)}) collective-permute-start(bf16[64,4096]{1,0:T(8,128)(2,1)S(1)} %slice.79), channel_id=1, source_target_pairs={{0,16},{16,0},{1,17},{17,1},{2,18},{18,2},{3,19},{19,3},{4,20},{20... | collective-permute-start | bytes 1572872 | tf_op jit(solution)/shard_map/ppermute | solution.py:20
  91.6 16.1 %copy-start.3 = (bf16[320,256]{1,0:T(8,128)(2,1)S(1)}, bf16[320,256]{1,0:T(8,128)(2,1)}, u32[]{:S(2)}) copy-start(bf16[320,256]{1,0:T(8,128)(2,1)} %param.11) | copy-start | bytes 491524
  91.6 16.1 %copy-start.4 = (bf16[320,256]{1,0:T(8,128)(2,1)S(1)}, bf16[320,256]{1,0:T(8,128)(2,1)}, u32[]{:S(2)}) copy-start(bf16[320,256]{1,0:T(8,128)(2,1)} %param.10) | copy-start | bytes 491524
  91.7 8.9 %collective-permute-start.2 = (bf16[24,4096]{1,0:T(8,128)(2,1)S(1)}, bf16[24,4096]{1,0:T(8,128)(2,1)S(1)}, u32[]{:S(2)}, u32[]{:S(2)}) collective-permute-start(bf16[24,4096]{1,0:T(8,128)(2,1)S(1)} %slice.57), channel_id=1, source_target_pairs={{0,2},{2,4},{4,6},{6,8},{8,10},{10,12},{12,14},{14,0},{1,3},{3,5},... | collective-permute-start | bytes 589832 | tf_op jit(solution)/shard_map/ppermute | solution.py:15
  95.2 7.4 %collective-permute-start.3 = (bf16[16,4096]{1,0:T(8,128)(2,1)S(1)}, bf16[16,4096]{1,0:T(8,128)(2,1)S(1)}, u32[]{:S(2)}, u32[]{:S(2)}) collective-permute-start(bf16[16,4096]{1,0:T(8,128)(2,1)S(1)} %slice.59), channel_id=1, source_target_pairs={{0,14},{2,0},{4,2},{6,4},{8,6},{10,8},{12,10},{14,12},{1,15},{3,1}... | collective-permute-start | bytes 393224 | tf_op jit(solution)/shard_map/ppermute | solution.py:15
  100.6 11.0 %collective-permute-start.5 = (bf16[8,4096]{1,0:T(8,128)(2,1)S(1)}, bf16[8,4096]{1,0:T(8,128)(2,1)S(1)}, u32[]{:S(2)}, u32[]{:S(2)}) collective-permute-start(bf16[8,4096]{1,0:T(8,128)(2,1)S(1)} %slice.80), channel_id=1, source_target_pairs={{0,10},{2,12},{4,14},{6,0},{8,2},{10,4},{12,6},{14,8},{1,11},{3,13... | collective-permute-start | bytes 196616 | tf_op jit(solution)/shard_map/ppermute | solution.py:15
  102.6 9.0 %collective-permute-start.4 = (bf16[8,4096]{1,0:T(8,128)(2,1)S(1)}, bf16[8,4096]{1,0:T(8,128)(2,1)S(1)}, u32[]{:S(2)}, u32[]{:S(2)}) collective-permute-start(bf16[8,4096]{1,0:T(8,128)(2,1)S(1)} %slice.81), channel_id=1, source_target_pairs={{0,6},{2,8},{4,10},{6,12},{8,14},{10,0},{12,2},{14,4},{1,7},{3,9},... | collective-permute-start | bytes 196616 | tf_op jit(solution)/shard_map/ppermute | solution.py:15
  (2 other events, 5.9 us)

commit v2 on v1

v2 whole, which is shorter than its diff:
```python
import functools
import math

import jax
import jax.numpy as jnp
from jax import lax
from jax.experimental import pallas as pl
from jax.experimental.pallas import tpu as pltpu
from jax.sharding import Mesh, PartitionSpec as P

REP = ("z", "xl")
FSDP = ("xh", "y", "core")
BF16 = jnp.bfloat16
F32 = jnp.float32
STEP = 2048


def shift(value, axis, step):
    n = lax.axis_size(axis)
    return lax.ppermute(value, axis, [(i, (i + step) % n) for i in range(n)])


def swap(value, axis, bit=1):
    n = lax.axis_size(axis)
    return lax.ppermute(value, axis, [(i, i ^ bit) for i in range(n)])


def picker(first, count):
    place = lax.broadcasted_iota(jnp.int32, (count, 256), 0) + first
    row = lax.broadcasted_iota(jnp.int32, (count, 256), 1)
    core = lax.axis_index("core") ^ (place >> 7)
    x = lax.axis_index("xh") ^ ((place >> 6) & 1)
    y = lax.axis_index("y") ^ ((place >> 5) & 1) ^ ((place >> 3) & 2) ^ ((place >> 1) & 4)
    wanted = (((x * 8 + y) * 2 + core) << 3) + (place & 7)
    return jnp.where(wanted == row, 1.0, 0.0).astype(BF16)


def across(a, b):
    return lax.dot_general(a, b, (((1,), (1,)), ((), ())), preferred_element_type=F32)


def fetch(copies):
    for copy in copies:
        copy.start()


def chunk_copies(cot, held, sems):
    return [
        pltpu.make_async_copy(
            cot.at[:, pl.ds(i * STEP, STEP)], held.at[:, pl.ds(i * STEP, STEP)], sems.at[i]
        )
        for i in range(held.shape[1] // STEP)
    ]


def part_kernel(cot, gate, up, send, keep, held, gate_held, up_held, sems, small_sems):
    small = [
        pltpu.make_async_copy(gate, gate_held, small_sems.at[0]),
        pltpu.make_async_copy(up, up_held, small_sems.at[1]),
    ]
    large = chunk_copies(cot, held, sems)
    fetch(small + large)
    pick = picker(0, 256)
    for copy in small:
        copy.wait()
    g = across(pick, gate_held[...])
    hidden = (g / (1.0 + jnp.exp(-g)) * across(pick, up_held[...])).astype(BF16)
    for i, copy in enumerate(large):
        copy.wait()
        here = pl.ds(i * STEP, STEP)
        total = jnp.dot(hidden, held[:, here], preferred_element_type=F32)
        keep[:, here] = total[:128]
        send[:, here] = total[128:].astype(BF16)


def add_kernel(keep, got, send, left):
    left[...] = keep[:64] + got[:64].astype(F32)
    send[...] = (keep[64:] + got[64:].astype(F32)).astype(BF16)


def factor_kernel(gate, up, by_gate, by_up):
    pick = picker(0, 256)
    g = across(gate[...], pick)
    u = across(up[...], pick)
    sigma = 1.0 / (1.0 + jnp.exp(-g))
    by_up[...] = g * sigma
    by_gate[...] = u * sigma * (1.0 + g * (1.0 - sigma))


def half_kernel(cot, mine, grad):
    grad[...] = across(cot[...], mine[...])


def grad_kernel(cot, other, grad, by_gate, by_up, grad_gate, grad_up):
    pick = picker(0, 256)
    total = jnp.concatenate([grad[...], across(cot[...], other[...])], axis=1)
    du = (total * by_up[...]).astype(BF16)
    dg = (total * by_gate[...]).astype(BF16)
    grad_up[...] = jnp.dot(du, pick, preferred_element_type=F32).astype(BF16)
    grad_gate[...] = jnp.dot(dg, pick, preferred_element_type=F32).astype(BF16)


def struct(rows, columns, dtype):
    return jax.ShapeDtypeStruct((rows, columns), dtype)


def cost(macs, nbytes):
    return pl.CostEstimate(flops=2 * macs, bytes_accessed=nbytes, transcendentals=0)


def outer_update(summed, replicas, old_momentum, base_rows):
    mean_delta = summed / replicas
    new_momentum = 0.9 * old_momentum + mean_delta
    new_params = base_rows - 0.7 * (mean_delta + 0.9 * new_momentum)
    return (new_params, new_momentum)


def per_device(
    cotangent, gate_pre, up_pre, slab_weight, base_params, momentum, codes, scales, frag_index
):
    tokens, width = cotangent.shape
    call = functools.partial(
        pl.pallas_call, compiler_params=pltpu.CompilerParams(vmem_limit_bytes=32 << 20)
    )
    chip = pl.BlockSpec(memory_space=pltpu.VMEM)
    far = pl.BlockSpec(memory_space=pltpu.HBM)
    chunks = width // STEP

    stored = [
        pltpu.with_memory_space_constraint(a, pltpu.HBM) for a in (cotangent, gate_pre, up_pre)
    ]

    rows = codes.shape[1]
    delta = codes[0].astype(F32).reshape(rows, width // 128, 128) * scales[0][..., None]
    delta = delta.reshape(rows, width)
    w_far = swap(slab_weight, "y", 4)
    left, right = delta[:, : width // 2], delta[:, width // 2 :]
    first = lax.axis_index("xl") == 0
    delta = jnp.where(first, left, right)
    z_far = swap(jnp.where(first, right, left), "xl")

    to_core, keep = call(
        part_kernel,
        in_specs=[far, far, far],
        out_specs=[chip, chip],
        out_shape=[struct(128, width, BF16), struct(128, width, F32)],
        scratch_shapes=[
            pltpu.VMEM((tokens, width), BF16),
            pltpu.VMEM((tokens, 256), BF16),
            pltpu.VMEM((tokens, 256), BF16),
            pltpu.SemaphoreType.DMA((chunks,)),
            pltpu.SemaphoreType.DMA((2,)),
        ],
        cost_estimate=cost(256 * width * tokens, 6 << 20),
    )(*stored)
    from_core = swap(to_core, "core")
    to_x, s = call(
        add_kernel,
        in_specs=[chip, chip],
        out_specs=[chip, chip],
        out_shape=[struct(64, width, BF16), struct(64, width, F32)],
        cost_estimate=cost(128 * width, 4 << 20),
    )(keep, from_core)
    barrier = lax.optimization_barrier
    from_x = swap(to_x, "xh")
    s, w, z = barrier((s, slab_weight, delta))
    z = z + z_far
    z_far = swap(z, "z", 1)
    w = jnp.concatenate([w, w_far])
    w_far = swap(w, "y", 2)
    z = z + z_far
    s, z = barrier((s, z))
    z_far = swap(z, "z", 2)

    s = s + from_x.astype(F32)
    from_y = swap(s[32:].astype(BF16), "y", 1)
    s, w, z = barrier((s, w, z))
    w = jnp.concatenate([w, w_far])
    w_far = swap(w, "y", 1)
    z = z + z_far
    z_far = swap(z, "z", 4)

    s = s[:32] + from_y.astype(F32)
    from_y = swap(s[16:].astype(BF16), "y", 2)
    s, w, z, gate_pre, up_pre = barrier((s, w, z, gate_pre, up_pre))
    w = jnp.concatenate([w, w_far])
    w_far = swap(w, "xh")
    by_gate, by_up = call(
        factor_kernel,
        in_specs=[chip, chip],
        out_specs=[chip, chip],
        out_shape=[struct(tokens, 256, F32)] * 2,
        cost_estimate=cost(256 * 512 * tokens, 1 << 20),
    )(gate_pre, up_pre)

    s = s[:16] + from_y.astype(F32)
    from_y = swap(s[8:].astype(BF16), "y", 4)
    s, z = barrier((s, z))
    z = z + z_far

    s = s[:8] + from_y.astype(F32)
    factor = 1.0 / math.sqrt(tokens * 32)
    inner_grad = (s * factor)[None]
    z_far = swap(z, "xl")
    z = jnp.where(first, jnp.concatenate([z, z_far], axis=1), jnp.concatenate([z_far, z], axis=1))

    mine = jnp.concatenate([w, w_far])
    other = swap(mine, "core")
    grad = call(
        half_kernel,
        in_specs=[chip, chip],
        out_specs=chip,
        out_shape=struct(tokens, 128, F32),
        cost_estimate=cost(128 * width * tokens, 16 << 20),
    )(cotangent, mine)
    grad_gate, grad_up = call(
        grad_kernel,
        in_specs=[chip, chip, chip, chip, chip],
        out_specs=[chip, chip],
        out_shape=[struct(tokens, 256, BF16)] * 2,
        cost_estimate=cost(128 * width * tokens, 4 << 20),
    )(cotangent, other, grad, by_gate, by_up)

    old_momentum = lax.dynamic_index_in_dim(momentum, frag_index[0], 0, keepdims=False)
    new_params, new_momentum = outer_update(z, 16, old_momentum, base_params)
    return (inner_grad, grad_gate, grad_up, new_params, new_momentum)


def solution(mesh):
    fine = Mesh(mesh.devices.reshape(8, 2, 2, 8, 2), REP + FSDP)
    tokens = P(REP + FSDP, None)
    return jax.shard_map(
        per_device,
        mesh=fine,
        in_specs=(
            tokens,
            tokens,
            tokens,
            P(FSDP, None),
            P(FSDP, None),
            P(None, FSDP, None),
            P(REP, FSDP, None),
            P(REP, FSDP, None),
            P(),
        ),
        out_specs=(P(REP, FSDP, None), tokens, tokens, P(FSDP, None), P(FSDP, None)),
        check_vma=False,
    )
```

time: 114 us -> 85.8 us (0.75)
  waiting for transfers between devices: 21.1 us -> 7.09 us
  matrix products: 8.48 us -> 0 us
  Pallas kernels: 0 us -> 7.44 us
  starting transfers between devices: 72.4 us -> 65.7 us
  local copies, waits for them, and re-layouts: 4.94 us -> 0.28 us
  other arithmetic: 3.46 us -> 1.76 us
    ppermute x8 -> x0, starting transfers between devices: 27.5 us -> none  [shift(): return lax.ppermute(value, axis, [(i, (i + step) % n) for i in range(n)])]
    ppermute x8 -> x15, starting transfers between devices: 44.9 us -> 65.7 us  [swap(): return lax.ppermute(value, axis, [(i, i ^ bit) for i in range(n)])]
    ppermute x8 -> x15, waiting for transfers between devices: 17.5 us -> 7.09 us  [swap(): return lax.ppermute(value, axis, [(i, i ^ bit) for i in range(n)])]
    dot_general x2 -> x0, matrix products: 8.48 us -> none  [the longest x1 4.63 us: per_device(): lax.dot_general(hidden_rel, cotangent, (((0,), (0,)), ((), ())), preferre...]
    pallas_call x0 -> x5, Pallas kernels: none -> 7.44 us  [the longest x1 4.24 us: per_device(): call(part_kernel, in_specs=[far, far, far], out_specs=[chip, chip], out_s...]
    ppermute x8 -> x0, waiting for transfers between devices: 3.57 us -> none  [shift(): return lax.ppermute(value, axis, [(i, (i + step) % n) for i in range(n)])]
    slice x6 -> x3, local copies, waits for them, and re-layouts: 2.85 us -> 0.05 us  [the longest x1 0.03 us: per_device(): from_y = swap(s[32:].astype(BF16), 'y', 1)]
    add x8 -> x7, other arithmetic: 1.76 us -> 0.21 us  [the longest x1 0.09 us: per_device(): s = s + from_x.astype(F32)]
  transfers between devices with their start and end apart: 16 -> 15, of which waited for: 5 -> 3; matrix products, arithmetic and copies ran while one was open for 6% -> 2% of each run, Pallas kernels for 0% -> 2%
where the time goes in v2:
time: 85.8 us; the launch traced here: 84.1 us
  starting transfers between devices  65.7 us (77%)
  Pallas kernels  7.44 us (9%)
  waiting for transfers between devices  7.09 us (8%)
  between operations  1.77 us (2%)
  other arithmetic  1.76 us (2%)
    ppermute x15, starting transfers between devices, swap(): return lax.ppermute(value, axis, [(i, i ^ bit) for i in range(n)])  65.7 us
    ppermute x15, waiting for transfers between devices, swap(): return lax.ppermute(value, axis, [(i, i ^ bit) for i in range(n)])  7.09 us
    pallas_call x1, Pallas kernels, per_device(): call(part_kernel, in_specs=[far, far, far], out_specs=[chip, chip], out_s...  4.24 us
    pallas_call x1, Pallas kernels, per_device(): call(grad_kernel, in_specs=[chip, chip, chip, chip, chip], out_specs=[chi...  1.82 us
  transfers between devices with their start and end apart: 15, of which 3 were waited for; matrix products, arithmetic and copies ran while one was open for 2% of the time, Pallas kernels for 2%

profile of v2, /device:TPU:1, one launch (start us, length us, event | category | flops | bytes accessed | tf_op | source)
XLA Modules:
  0.0 84.1 jit_solution(5028521222220970600)
XLA Ops:
  0.7 4.2 %shard_map.128 = (bf16[128,4096]{1,0:T(8,128)(2,1)}, f32[128,4096]{1,0:T(8,128)S(1)}) custom-call(bf16[320,4096]{1,0:T(8,128)(2,1)} %cot.5, bf16[320,256]{1,0:T(8,128)(2,1)} %gate.2, bf16[320,256]{1,0:T(8,128)(2,1)} %up.2), custom_call_target="tpu_custom_call" | custom-call | flops 671088640 | bytes 6291456 | tf_op jit(solution)/shard_map/pallas_call | solution.py:142
  4.9 8.8 %collective-permute-start = (bf16[128,4096]{1,0:T(8,128)(2,1)}, bf16[128,4096]{1,0:T(8,128)(2,1)S(1)}, u32[]{:S(2)}, u32[]{:S(2)}) collective-permute-start(bf16[128,4096]{1,0:T(8,128)(2,1)} %get-tuple-element.29), channel_id=1, source_target_pairs={{0,1},{1,0},{2,3},{3,2},{4,5},{5,4},{6,7},{7,6},{8,9},{9,8},{10,11... | collective-permute-start | bytes 3145736 | tf_op jit(solution)/shard_map/ppermute | solution.py:25
  13.9 1.9 %collective-permute-start.1 = (f32[8,2048]{1,0:T(8,128)S(1)}, f32[8,2048]{1,0:T(8,128)S(1)}, u32[]{:S(2)}, u32[]{:S(2)}) collective-permute-start(f32[8,2048]{1,0:T(8,128)S(1)} %get-tuple-element.53), channel_id=1, source_target_pairs={{0,32},{32,0},{1,33},{33,1},{2,34},{34,2},{3,35},{35,3},{4,36},{36... | collective-permute-start | bytes 196616 | tf_op jit(solution)/shard_map/ppermute | solution.py:25
  15.9 3.3 %collective-permute-start.4 = (bf16[8,4096]{1,0:T(8,128)(2,1)S(1)}, bf16[8,4096]{1,0:T(8,128)(2,1)S(1)}, u32[]{:S(2)}, u32[]{:S(2)}) collective-permute-start(bf16[8,4096]{1,0:T(8,128)(2,1)S(1)} %copy-done.6), channel_id=1, source_target_pairs={{0,8},{2,10},{4,12},{6,14},{8,0},{10,2},{12,4},{14,6},{1,9},{3,11}... | collective-permute-start | bytes 196616 | tf_op jit(solution)/shard_map/ppermute | solution.py:25
  20.0 4.0 %collective-permute-start.2 = (f32[8,2048]{1,0:T(8,128)S(1)}, f32[8,2048]{1,0:T(8,128)S(1)}, u32[]{:S(2)}, u32[]{:S(2)}) collective-permute-start(f32[8,2048]{1,0:T(8,128)S(1)} %add.34), channel_id=1, source_target_pairs={{0,64},{64,0},{128,192},{192,128},{256,320},{320,256},{384,448},{4... | collective-permute-start | bytes 196616 | tf_op jit(solution)/shard_map/ppermute | solution.py:25
  24.0 4.4 %collective-permute-start.3 = (bf16[64,4096]{1,0:T(8,128)(2,1)S(1)}, bf16[64,4096]{1,0:T(8,128)(2,1)S(1)}, u32[]{:S(2)}, u32[]{:S(2)}) collective-permute-start(bf16[64,4096]{1,0:T(8,128)(2,1)S(1)} %get-tuple-element.34), channel_id=1, source_target_pairs={{0,16},{16,0},{1,17},{17,1},{2,18},{18,2},{3,19},{19,3},{4,20},{20... | collective-permute-start | bytes 1572872 | tf_op jit(solution)/shard_map/ppermute | solution.py:25
  28.4 2.4 %collective-permute-start.6 = (bf16[16,4096]{1,0:T(8,128)(2,1)S(1)}, bf16[16,4096]{1,0:T(8,128)(2,1)S(1)}, u32[]{:S(2)}, u32[]{:S(2)}) collective-permute-start(bf16[16,4096]{1,0:T(8,128)(2,1)S(1)} %constant_dynamic-update-slice_fusion), channel_id=1, source_target_pairs={{0,4},{2,6},{4,0},{6,2},{8,12},{10,14},{12,8},{14,10},{1,5},{3,7},... | collective-permute-start | bytes 393224 | tf_op jit(solution)/shard_map/ppermute | solution.py:25
  30.9 5.8 %collective-permute-start.7 = (f32[8,2048]{1,0:T(8,128)S(1)}, f32[8,2048]{1,0:T(8,128)S(1)}, u32[]{:S(2)}, u32[]{:S(2)}) collective-permute-start(f32[8,2048]{1,0:T(8,128)S(1)} %add.35), channel_id=1, source_target_pairs={{0,128},{64,192},{128,0},{192,64},{256,384},{320,448},{384,256},{4... | collective-permute-start | bytes 196616 | tf_op jit(solution)/shard_map/ppermute | solution.py:25
  36.7 3.3 %collective-permute-done.3 = bf16[64,4096]{1,0:T(8,128)(2,1)S(1)} collective-permute-done((bf16[64,4096]{1,0:T(8,128)(2,1)S(1)}, bf16[64,4096]{1,0:T(8,128)(2,1)S(1)}, u32[]{:S(2)}, u32[]{:S(2)}) %collective-permute-start.3) | collective-permute-done | bytes 524320 | tf_op jit(solution)/shard_map/ppermute | solution.py:25
  40.2 2.4 %collective-permute-start.5 = (bf16[32,4096]{1,0:T(8,128)(2,1)S(1)}, bf16[32,4096]{1,0:T(8,128)(2,1)S(1)}, u32[]{:S(2)}, u32[]{:S(2)}) collective-permute-start(bf16[32,4096]{1,0:T(8,128)(2,1)S(1)} %slice.50), channel_id=1, source_target_pairs={{0,2},{2,0},{4,6},{6,4},{8,10},{10,8},{12,14},{14,12},{1,3},{3,1},... | collective-permute-start | bytes 786440 | tf_op jit(solution)/shard_map/ppermute | solution.py:25
  42.7 9.7 %collective-permute-start.13 = (f32[8,2048]{1,0:T(8,128)S(1)}, f32[8,2048]{1,0:T(8,128)S(1)}, u32[]{:S(2)}, u32[]{:S(2)}) collective-permute-start(f32[8,2048]{1,0:T(8,128)S(1)} %add.38), channel_id=1, source_target_pairs={{0,256},{64,320},{128,384},{192,448},{256,0},{320,64},{384,128},{4... | collective-permute-start | bytes 196616 | tf_op jit(solution)/shard_map/ppermute | solution.py:25
  52.4 3.0 %collective-permute-start.10 = (bf16[32,4096]{1,0:T(8,128)(2,1)S(1)}, bf16[32,4096]{1,0:T(8,128)(2,1)S(1)}, u32[]{:S(2)}, u32[]{:S(2)}) collective-permute-start(bf16[32,4096]{1,0:T(8,128)(2,1)S(1)} %constant_dynamic-update-slice_fusion.2), channel_id=1, source_target_pairs={{0,2},{2,0},{4,6},{6,4},{8,10},{10,8},{12,14},{14,12},{1,3},{3,1},... | collective-permute-start | bytes 786440 | tf_op jit(solution)/shard_map/ppermute | solution.py:25
  55.5 2.7 %collective-permute-start.8 = (bf16[16,4096]{1,0:T(8,128)(2,1)S(1)}, bf16[16,4096]{1,0:T(8,128)(2,1)S(1)}, u32[]{:S(2)}, u32[]{:S(2)}) collective-permute-start(bf16[16,4096]{1,0:T(8,128)(2,1)S(1)} %slice.51), channel_id=1, source_target_pairs={{0,4},{2,6},{4,0},{6,2},{8,12},{10,14},{12,8},{14,10},{1,5},{3,7},... | collective-permute-start | bytes 393224 | tf_op jit(solution)/shard_map/ppermute | solution.py:25
  58.3 1.3 %collective-permute-done.10 = bf16[32,4096]{1,0:T(8,128)(2,1)S(1)} collective-permute-done((bf16[32,4096]{1,0:T(8,128)(2,1)S(1)}, bf16[32,4096]{1,0:T(8,128)(2,1)S(1)}, u32[]{:S(2)}, u32[]{:S(2)}) %collective-permute-start.10) | collective-permute-done | bytes 262176 | tf_op jit(solution)/shard_map/ppermute | solution.py:25
  59.6 4.4 %collective-permute-start.11 = (bf16[64,4096]{1,0:T(8,128)(2,1)S(1)}, bf16[64,4096]{1,0:T(8,128)(2,1)S(1)}, u32[]{:S(2)}, u32[]{:S(2)}) collective-permute-start(bf16[64,4096]{1,0:T(8,128)(2,1)S(1)} %pad_maximum_fusion), channel_id=1, source_target_pairs={{0,16},{16,0},{1,17},{17,1},{2,18},{18,2},{3,19},{19,3},{4,20},{20... | collective-permute-start | bytes 1572872 | tf_op jit(solution)/shard_map/ppermute | solution.py:25
  64.0 0.4 shard_map.131
  64.5 1.9 %collective-permute-start.14 = (f32[8,2048]{1,0:T(8,128)S(1)}, f32[8,2048]{1,0:T(8,128)S(1)}, u32[]{:S(2)}, u32[]{:S(2)}) collective-permute-start(f32[8,2048]{1,0:T(8,128)S(1)} %add.41), channel_id=1, source_target_pairs={{0,32},{32,0},{1,33},{33,1},{2,34},{34,2},{3,35},{35,3},{4,36},{36... | collective-permute-start | bytes 196616 | tf_op jit(solution)/shard_map/ppermute | solution.py:25
  66.4 2.6 %collective-permute-start.9 = (bf16[8,4096]{1,0:T(8,128)(2,1)S(1)}, bf16[8,4096]{1,0:T(8,128)(2,1)S(1)}, u32[]{:S(2)}, u32[]{:S(2)}) collective-permute-start(bf16[8,4096]{1,0:T(8,128)(2,1)S(1)} %slice.52), channel_id=1, source_target_pairs={{0,8},{2,10},{4,12},{6,14},{8,0},{10,2},{12,4},{14,6},{1,9},{3,11}... | collective-permute-start | bytes 196616 | tf_op jit(solution)/shard_map/ppermute | solution.py:25
  69.0 2.5 %collective-permute-done.11 = bf16[64,4096]{1,0:T(8,128)(2,1)S(1)} collective-permute-done((bf16[64,4096]{1,0:T(8,128)(2,1)S(1)}, bf16[64,4096]{1,0:T(8,128)(2,1)S(1)}, u32[]{:S(2)}, u32[]{:S(2)}) %collective-permute-start.11) | collective-permute-done | bytes 524320 | tf_op jit(solution)/shard_map/ppermute | solution.py:25
  71.5 8.4 %collective-permute-start.12 = (bf16[128,4096]{1,0:T(8,128)(2,1)S(1)}, bf16[128,4096]{1,0:T(8,128)(2,1)S(1)}, u32[]{:S(2)}, u32[]{:S(2)}) collective-permute-start(bf16[128,4096]{1,0:T(8,128)(2,1)S(1)} %constant_dynamic-update-slice_fusion.4.mine), channel_id=1, source_target_pairs={{0,1},{1,0},{2,3},{3,2},{4,5},{5,4},{6,7},{7,6},{8,9},{9,8},{10,11... | collective-permute-start | bytes 3145736 | tf_op jit(solution)/shard_map/ppermute | solution.py:25
  80.0 0.7 multiply_bitcast_fusion
  80.7 0.7 multiply_subtract_fusion
  81.4 0.8 shard_map.130.grad
  82.3 1.8 %shard_map.132 = (bf16[320,256]{1,0:T(8,128)(2,1)}, bf16[320,256]{1,0:T(8,128)(2,1)}) custom-call(bf16[320,4096]{1,0:T(8,128)(2,1)S(1)} %copy-done, bf16[128,4096]{1,0:T(8,128)(2,1)S(1)} %collective-permute-done.12.other, f32[320,128]{1,0:T(8,128)S(1)} %shard_map.130.grad, f32[320,256]{1,0:T(8,128)S(1)} %get-tuple-element.46.by_gate, ...), custom_call_target="tpu_custom_call" | custom-call | flops 335544320 | bytes 4194304 | tf_op jit(solution)/shard_map/pallas_call | solution.py:216
  (50 shorter events, 0.8 us)
Async XLA Ops:
  0.6 13.1 %copy-start.7 = (f32[1,8,32]{2,1,0:T(8,128)S(1)}, f32[1,8,32]{2,1,0:T(8,128)}, u32[]{:S(2)}) copy-start(f32[1,8,32]{2,1,0:T(8,128)} %param.16) | copy-start | bytes 3076
  0.6 13.2 %copy-start.4 = (s32[1,8,4096]{2,1,0:T(8,128)S(1)}, s32[1,8,4096]{2,1,0:T(8,128)}, u32[]{:S(2)}) copy-start(s32[1,8,4096]{2,1,0:T(8,128)} %param.15) | copy-start | bytes 393220
  0.7 15.2 %copy-start.6 = (bf16[8,4096]{1,0:T(8,128)(2,1)S(1)}, bf16[8,4096]{1,0:T(8,128)(2,1)}, u32[]{:S(2)}) copy-start(bf16[8,4096]{1,0:T(8,128)(2,1)} %param.12) | copy-start | bytes 196612
  4.9 14.9 %collective-permute-start = (bf16[128,4096]{1,0:T(8,128)(2,1)}, bf16[128,4096]{1,0:T(8,128)(2,1)S(1)}, u32[]{:S(2)}, u32[]{:S(2)}) collective-permute-start(bf16[128,4096]{1,0:T(8,128)(2,1)} %get-tuple-element.29), channel_id=1, source_target_pairs={{0,1},{1,0},{2,3},{3,2},{4,5},{5,4},{6,7},{7,6},{8,9},{9,8},{10,11... | collective-permute-start | bytes 3145736 | tf_op jit(solution)/shard_map/ppermute | solution.py:25
  13.9 6.1 %collective-permute-start.1 = (f32[8,2048]{1,0:T(8,128)S(1)}, f32[8,2048]{1,0:T(8,128)S(1)}, u32[]{:S(2)}, u32[]{:S(2)}) collective-permute-start(f32[8,2048]{1,0:T(8,128)S(1)} %get-tuple-element.53), channel_id=1, source_target_pairs={{0,32},{32,0},{1,33},{33,1},{2,34},{34,2},{3,35},{35,3},{4,36},{36... | collective-permute-start | bytes 196616 | tf_op jit(solution)/shard_map/ppermute | solution.py:25
  15.9 12.5 %collective-permute-start.4 = (bf16[8,4096]{1,0:T(8,128)(2,1)S(1)}, bf16[8,4096]{1,0:T(8,128)(2,1)S(1)}, u32[]{:S(2)}, u32[]{:S(2)}) collective-permute-start(bf16[8,4096]{1,0:T(8,128)(2,1)S(1)} %copy-done.6), channel_id=1, source_target_pairs={{0,8},{2,10},{4,12},{6,14},{8,0},{10,2},{12,4},{14,6},{1,9},{3,11}... | collective-permute-start | bytes 196616 | tf_op jit(solution)/shard_map/ppermute | solution.py:25
  20.0 10.8 %collective-permute-start.2 = (f32[8,2048]{1,0:T(8,128)S(1)}, f32[8,2048]{1,0:T(8,128)S(1)}, u32[]{:S(2)}, u32[]{:S(2)}) collective-permute-start(f32[8,2048]{1,0:T(8,128)S(1)} %add.34), channel_id=1, source_target_pairs={{0,64},{64,0},{128,192},{192,128},{256,320},{320,256},{384,448},{4... | collective-permute-start | bytes 196616 | tf_op jit(solution)/shard_map/ppermute | solution.py:25
  24.0 16.0 %collective-permute-start.3 = (bf16[64,4096]{1,0:T(8,128)(2,1)S(1)}, bf16[64,4096]{1,0:T(8,128)(2,1)S(1)}, u32[]{:S(2)}, u32[]{:S(2)}) collective-permute-start(bf16[64,4096]{1,0:T(8,128)(2,1)S(1)} %get-tuple-element.34), channel_id=1, source_target_pairs={{0,16},{16,0},{1,17},{17,1},{2,18},{18,2},{3,19},{19,3},{4,20},{20... | collective-permute-start | bytes 1572872 | tf_op jit(solution)/shard_map/ppermute | solution.py:25
  28.4 24.0 %collective-permute-start.6 = (bf16[16,4096]{1,0:T(8,128)(2,1)S(1)}, bf16[16,4096]{1,0:T(8,128)(2,1)S(1)}, u32[]{:S(2)}, u32[]{:S(2)}) collective-permute-start(bf16[16,4096]{1,0:T(8,128)(2,1)S(1)} %constant_dynamic-update-slice_fusion), channel_id=1, source_target_pairs={{0,4},{2,6},{4,0},{6,2},{8,12},{10,14},{12,8},{14,10},{1,5},{3,7},... | collective-permute-start | bytes 393224 | tf_op jit(solution)/shard_map/ppermute | solution.py:25
  30.9 11.7 %collective-permute-start.7 = (f32[8,2048]{1,0:T(8,128)S(1)}, f32[8,2048]{1,0:T(8,128)S(1)}, u32[]{:S(2)}, u32[]{:S(2)}) collective-permute-start(f32[8,2048]{1,0:T(8,128)S(1)} %add.35), channel_id=1, source_target_pairs={{0,128},{64,192},{128,0},{192,64},{256,384},{320,448},{384,256},{4... | collective-permute-start | bytes 196616 | tf_op jit(solution)/shard_map/ppermute | solution.py:25
  40.1 23.9 %copy-start.1 = (bf16[320,256]{1,0:T(8,128)(2,1)S(1)}, bf16[320,256]{1,0:T(8,128)(2,1)}, u32[]{:S(2)}) copy-start(bf16[320,256]{1,0:T(8,128)(2,1)} %gate.2) | copy-start | bytes 491524
  40.1 23.9 %copy-start.2 = (bf16[320,256]{1,0:T(8,128)(2,1)S(1)}, bf16[320,256]{1,0:T(8,128)(2,1)}, u32[]{:S(2)}) copy-start(bf16[320,256]{1,0:T(8,128)(2,1)} %up.2) | copy-start | bytes 491524
  40.2 15.2 %collective-permute-start.5 = (bf16[32,4096]{1,0:T(8,128)(2,1)S(1)}, bf16[32,4096]{1,0:T(8,128)(2,1)S(1)}, u32[]{:S(2)}, u32[]{:S(2)}) collective-permute-start(bf16[32,4096]{1,0:T(8,128)(2,1)S(1)} %slice.50), channel_id=1, source_target_pairs={{0,2},{2,0},{4,6},{6,4},{8,10},{10,8},{12,14},{14,12},{1,3},{3,1},... | collective-permute-start | bytes 786440 | tf_op jit(solution)/shard_map/ppermute | solution.py:25
  42.7 21.8 %collective-permute-start.13 = (f32[8,2048]{1,0:T(8,128)S(1)}, f32[8,2048]{1,0:T(8,128)S(1)}, u32[]{:S(2)}, u32[]{:S(2)}) collective-permute-start(f32[8,2048]{1,0:T(8,128)S(1)} %add.38), channel_id=1, source_target_pairs={{0,256},{64,320},{128,384},{192,448},{256,0},{320,64},{384,128},{4... | collective-permute-start | bytes 196616 | tf_op jit(solution)/shard_map/ppermute | solution.py:25
  52.4 7.1 %collective-permute-start.10 = (bf16[32,4096]{1,0:T(8,128)(2,1)S(1)}, bf16[32,4096]{1,0:T(8,128)(2,1)S(1)}, u32[]{:S(2)}, u32[]{:S(2)}) collective-permute-start(bf16[32,4096]{1,0:T(8,128)(2,1)S(1)} %constant_dynamic-update-slice_fusion.2), channel_id=1, source_target_pairs={{0,2},{2,0},{4,6},{6,4},{8,10},{10,8},{12,14},{14,12},{1,3},{3,1},... | collective-permute-start | bytes 786440 | tf_op jit(solution)/shard_map/ppermute | solution.py:25
  55.5 25.2 %copy-start.3 = (f32[8,4096]{1,0:T(8,128)S(1)}, f32[8,4096]{1,0:T(8,128)}, u32[]{:S(2)}) copy-start(f32[8,4096]{1,0:T(8,128)} %param.13) | copy-start | bytes 393220
  55.5 25.2 %copy-start.5 = (f32[2,8,4096]{2,1,0:T(8,128)S(1)}, f32[2,8,4096]{2,1,0:T(8,128)}, u32[]{:S(2)}) copy-start(f32[2,8,4096]{2,1,0:T(8,128)} %param.14) | copy-start | bytes 786436
  55.5 25.9 %copy-start = (bf16[320,4096]{1,0:T(8,128)(2,1)S(1)}, bf16[320,4096]{1,0:T(8,128)(2,1)}, u32[]{:S(2)}) copy-start(bf16[320,4096]{1,0:T(8,128)(2,1)} %cot.5) | copy-start | bytes 7864324
  55.5 8.8 %collective-permute-start.8 = (bf16[16,4096]{1,0:T(8,128)(2,1)S(1)}, bf16[16,4096]{1,0:T(8,128)(2,1)S(1)}, u32[]{:S(2)}, u32[]{:S(2)}) collective-permute-start(bf16[16,4096]{1,0:T(8,128)(2,1)S(1)} %slice.51), channel_id=1, source_target_pairs={{0,4},{2,6},{4,0},{6,2},{8,12},{10,14},{12,8},{14,10},{1,5},{3,7},... | collective-permute-start | bytes 393224 | tf_op jit(solution)/shard_map/ppermute | solution.py:25
  59.6 11.9 %collective-permute-start.11 = (bf16[64,4096]{1,0:T(8,128)(2,1)S(1)}, bf16[64,4096]{1,0:T(8,128)(2,1)S(1)}, u32[]{:S(2)}, u32[]{:S(2)}) collective-permute-start(bf16[64,4096]{1,0:T(8,128)(2,1)S(1)} %pad_maximum_fusion), channel_id=1, source_target_pairs={{0,16},{16,0},{1,17},{17,1},{2,18},{18,2},{3,19},{19,3},{4,20},{20... | collective-permute-start | bytes 1572872 | tf_op jit(solution)/shard_map/ppermute | solution.py:25
  64.5 16.2 %collective-permute-start.14 = (f32[8,2048]{1,0:T(8,128)S(1)}, f32[8,2048]{1,0:T(8,128)S(1)}, u32[]{:S(2)}, u32[]{:S(2)}) collective-permute-start(f32[8,2048]{1,0:T(8,128)S(1)} %add.41), channel_id=1, source_target_pairs={{0,32},{32,0},{1,33},{33,1},{2,34},{34,2},{3,35},{35,3},{4,36},{36... | collective-permute-start | bytes 196616 | tf_op jit(solution)/shard_map/ppermute | solution.py:25
  66.4 13.6 %collective-permute-start.9 = (bf16[8,4096]{1,0:T(8,128)(2,1)S(1)}, bf16[8,4096]{1,0:T(8,128)(2,1)S(1)}, u32[]{:S(2)}, u32[]{:S(2)}) collective-permute-start(bf16[8,4096]{1,0:T(8,128)(2,1)S(1)} %slice.52), channel_id=1, source_target_pairs={{0,8},{2,10},{4,12},{6,14},{8,0},{10,2},{12,4},{14,6},{1,9},{3,11}... | collective-permute-start | bytes 196616 | tf_op jit(solution)/shard_map/ppermute | solution.py:25
  71.5 10.7 %collective-permute-start.12 = (bf16[128,4096]{1,0:T(8,128)(2,1)S(1)}, bf16[128,4096]{1,0:T(8,128)(2,1)S(1)}, u32[]{:S(2)}, u32[]{:S(2)}) collective-permute-start(bf16[128,4096]{1,0:T(8,128)(2,1)S(1)} %constant_dynamic-update-slice_fusion.4.mine), channel_id=1, source_target_pairs={{0,1},{1,0},{2,3},{3,2},{4,5},{5,4},{6,7},{7,6},{8,9},{9,8},{10,11... | collective-permute-start | bytes 3145736 | tf_op jit(solution)/shard_map/ppermute | solution.py:25

commit v3 on v2

--- a/solution.py
+++ b/solution.py
@@ -120,7 +120,7 @@
 ):
     tokens, width = cotangent.shape
     call = functools.partial(
-        pl.pallas_call, compiler_params=pltpu.CompilerParams(vmem_limit_bytes=32 << 20)
+        pl.pallas_call, compiler_params=pltpu.CompilerParams(vmem_limit_bytes=16 << 20)
     )
     chip = pl.BlockSpec(memory_space=pltpu.VMEM)
     far = pl.BlockSpec(memory_space=pltpu.HBM)
@@ -135,9 +135,9 @@
     delta = delta.reshape(rows, width)
     w_far = swap(slab_weight, "y", 4)
     left, right = delta[:, : width // 2], delta[:, width // 2 :]
-    first = lax.axis_index("xl") == 0
+    first = lax.axis_index("z") % 2 == 0
     delta = jnp.where(first, left, right)
-    z_far = swap(jnp.where(first, right, left), "xl")
+    z_far = swap(jnp.where(first, right, left), "z", 1)
 
     to_core, keep = call(
         part_kernel,
@@ -165,7 +165,7 @@
     from_x = swap(to_x, "xh")
     s, w, z = barrier((s, slab_weight, delta))
     z = z + z_far
-    z_far = swap(z, "z", 1)
+    z_far = swap(z, "xl")
     w = jnp.concatenate([w, w_far])
     w_far = swap(w, "y", 2)
     z = z + z_far
@@ -201,7 +201,7 @@
     s = s[:8] + from_y.astype(F32)
     factor = 1.0 / math.sqrt(tokens * 32)
     inner_grad = (s * factor)[None]
-    z_far = swap(z, "xl")
+    z_far = swap(z, "z", 1)
     z = jnp.where(first, jnp.concatenate([z, z_far], axis=1), jnp.concatenate([z_far, z], axis=1))
 
     mine = jnp.concatenate([w, w_far])

time: 85.8 us -> 82.7 us (0.964); the launches traced: 84.1 us -> 82.1 us
  starting transfers between devices: 65.7 us -> 63.5 us
    ppermute x15, starting transfers between devices: 65.7 us -> 63.5 us  [swap(): return lax.ppermute(value, axis, [(i, i ^ bit) for i in range(n)])]
where the time goes in v3:
time: 82.7 us; the launch traced here: 82.1 us
  starting transfers between devices  63.5 us (77%)
  Pallas kernels  7.44 us (9%)
  waiting for transfers between devices  7.36 us (9%)
  other arithmetic  1.77 us (2%)
  between operations  1.77 us (2%)
    ppermute x15, starting transfers between devices, swap(): return lax.ppermute(value, axis, [(i, i ^ bit) for i in range(n)])  63.5 us
    ppermute x15, waiting for transfers between devices, swap(): return lax.ppermute(value, axis, [(i, i ^ bit) for i in range(n)])  7.36 us
    pallas_call x1, Pallas kernels, per_device(): call(part_kernel, in_specs=[far, far, far], out_specs=[chip, chip], out_s...  4.24 us
    pallas_call x1, Pallas kernels, per_device(): call(grad_kernel, in_specs=[chip, chip, chip, chip, chip], out_specs=[chi...  1.82 us
  transfers between devices with their start and end apart: 15, of which 3 were waited for; matrix products, arithmetic and copies ran while one was open for 2% of the time, Pallas kernels for 2%

profile of v3, /device:TPU:1, one launch (start us, length us, event | category | flops | bytes accessed | tf_op | source)
XLA Modules:
  0.0 82.1 jit_solution(5650434890933638401)
XLA Ops:
  0.7 4.2 %shard_map.128 = (bf16[128,4096]{1,0:T(8,128)(2,1)}, f32[128,4096]{1,0:T(8,128)S(1)}) custom-call(bf16[320,4096]{1,0:T(8,128)(2,1)} %cot.5, bf16[320,256]{1,0:T(8,128)(2,1)} %gate.2, bf16[320,256]{1,0:T(8,128)(2,1)} %up.2), custom_call_target="tpu_custom_call" | custom-call | flops 671088640 | bytes 6291456 | tf_op jit(solution)/shard_map/pallas_call | solution.py:142
  4.9 8.8 %collective-permute-start = (bf16[128,4096]{1,0:T(8,128)(2,1)}, bf16[128,4096]{1,0:T(8,128)(2,1)S(1)}, u32[]{:S(2)}, u32[]{:S(2)}) collective-permute-start(bf16[128,4096]{1,0:T(8,128)(2,1)} %get-tuple-element.29), channel_id=1, source_target_pairs={{0,1},{1,0},{2,3},{3,2},{4,5},{5,4},{6,7},{7,6},{8,9},{9,8},{10,11... | collective-permute-start | bytes 3145736 | tf_op jit(solution)/shard_map/ppermute | solution.py:25
  13.9 1.9 %collective-permute-start.1 = (f32[8,2048]{1,0:T(8,128)S(1)}, f32[8,2048]{1,0:T(8,128)S(1)}, u32[]{:S(2)}, u32[]{:S(2)}) collective-permute-start(f32[8,2048]{1,0:T(8,128)S(1)} %get-tuple-element.53), channel_id=1, source_target_pairs={{0,64},{64,0},{128,192},{192,128},{256,320},{320,256},{384,448},{4... | collective-permute-start | bytes 196616 | tf_op jit(solution)/shard_map/ppermute | solution.py:25
  15.9 4.2 %collective-permute-start.4 = (bf16[8,4096]{1,0:T(8,128)(2,1)S(1)}, bf16[8,4096]{1,0:T(8,128)(2,1)S(1)}, u32[]{:S(2)}, u32[]{:S(2)}) collective-permute-start(bf16[8,4096]{1,0:T(8,128)(2,1)S(1)} %copy-done.6), channel_id=1, source_target_pairs={{0,8},{2,10},{4,12},{6,14},{8,0},{10,2},{12,4},{14,6},{1,9},{3,11}... | collective-permute-start | bytes 196616 | tf_op jit(solution)/shard_map/ppermute | solution.py:25
  20.9 3.1 %collective-permute-start.2 = (f32[8,2048]{1,0:T(8,128)S(1)}, f32[8,2048]{1,0:T(8,128)S(1)}, u32[]{:S(2)}, u32[]{:S(2)}) collective-permute-start(f32[8,2048]{1,0:T(8,128)S(1)} %add.39), channel_id=1, source_target_pairs={{0,32},{32,0},{1,33},{33,1},{2,34},{34,2},{3,35},{35,3},{4,36},{36... | collective-permute-start | bytes 196616 | tf_op jit(solution)/shard_map/ppermute | solution.py:25
  24.0 4.4 %collective-permute-start.3 = (bf16[64,4096]{1,0:T(8,128)(2,1)S(1)}, bf16[64,4096]{1,0:T(8,128)(2,1)S(1)}, u32[]{:S(2)}, u32[]{:S(2)}) collective-permute-start(bf16[64,4096]{1,0:T(8,128)(2,1)S(1)} %get-tuple-element.34), channel_id=1, source_target_pairs={{0,16},{16,0},{1,17},{17,1},{2,18},{18,2},{3,19},{19,3},{4,20},{20... | collective-permute-start | bytes 1572872 | tf_op jit(solution)/shard_map/ppermute | solution.py:25
  28.4 2.4 %collective-permute-start.6 = (bf16[16,4096]{1,0:T(8,128)(2,1)S(1)}, bf16[16,4096]{1,0:T(8,128)(2,1)S(1)}, u32[]{:S(2)}, u32[]{:S(2)}) collective-permute-start(bf16[16,4096]{1,0:T(8,128)(2,1)S(1)} %constant_dynamic-update-slice_fusion), channel_id=1, source_target_pairs={{0,4},{2,6},{4,0},{6,2},{8,12},{10,14},{12,8},{14,10},{1,5},{3,7},... | collective-permute-start | bytes 393224 | tf_op jit(solution)/shard_map/ppermute | solution.py:25
  30.9 5.8 %collective-permute-start.7 = (f32[8,2048]{1,0:T(8,128)S(1)}, f32[8,2048]{1,0:T(8,128)S(1)}, u32[]{:S(2)}, u32[]{:S(2)}) collective-permute-start(f32[8,2048]{1,0:T(8,128)S(1)} %add.40), channel_id=1, source_target_pairs={{0,128},{64,192},{128,0},{192,64},{256,384},{320,448},{384,256},{4... | collective-permute-start | bytes 196616 | tf_op jit(solution)/shard_map/ppermute | solution.py:25
  36.7 3.3 %collective-permute-done.3 = bf16[64,4096]{1,0:T(8,128)(2,1)S(1)} collective-permute-done((bf16[64,4096]{1,0:T(8,128)(2,1)S(1)}, bf16[64,4096]{1,0:T(8,128)(2,1)S(1)}, u32[]{:S(2)}, u32[]{:S(2)}) %collective-permute-start.3) | collective-permute-done | bytes 524320 | tf_op jit(solution)/shard_map/ppermute | solution.py:25
  40.2 2.4 %collective-permute-start.5 = (bf16[32,4096]{1,0:T(8,128)(2,1)S(1)}, bf16[32,4096]{1,0:T(8,128)(2,1)S(1)}, u32[]{:S(2)}, u32[]{:S(2)}) collective-permute-start(bf16[32,4096]{1,0:T(8,128)(2,1)S(1)} %slice.50), channel_id=1, source_target_pairs={{0,2},{2,0},{4,6},{6,4},{8,10},{10,8},{12,14},{14,12},{1,3},{3,1},... | collective-permute-start | bytes 786440 | tf_op jit(solution)/shard_map/ppermute | solution.py:25
  42.7 3.0 %collective-permute-start.10 = (bf16[32,4096]{1,0:T(8,128)(2,1)S(1)}, bf16[32,4096]{1,0:T(8,128)(2,1)S(1)}, u32[]{:S(2)}, u32[]{:S(2)}) collective-permute-start(bf16[32,4096]{1,0:T(8,128)(2,1)S(1)} %constant_dynamic-update-slice_fusion.2), channel_id=1, source_target_pairs={{0,2},{2,0},{4,6},{6,4},{8,10},{10,8},{12,14},{14,12},{1,3},{3,1},... | collective-permute-start | bytes 786440 | tf_op jit(solution)/shard_map/ppermute | solution.py:25
  45.7 9.7 %collective-permute-start.13 = (f32[8,2048]{1,0:T(8,128)S(1)}, f32[8,2048]{1,0:T(8,128)S(1)}, u32[]{:S(2)}, u32[]{:S(2)}) collective-permute-start(f32[8,2048]{1,0:T(8,128)S(1)} %add.43), channel_id=1, source_target_pairs={{0,256},{64,320},{128,384},{192,448},{256,0},{320,64},{384,128},{4... | collective-permute-start | bytes 196616 | tf_op jit(solution)/shard_map/ppermute | solution.py:25
  55.5 2.7 %collective-permute-start.8 = (bf16[16,4096]{1,0:T(8,128)(2,1)S(1)}, bf16[16,4096]{1,0:T(8,128)(2,1)S(1)}, u32[]{:S(2)}, u32[]{:S(2)}) collective-permute-start(bf16[16,4096]{1,0:T(8,128)(2,1)S(1)} %slice.51), channel_id=1, source_target_pairs={{0,4},{2,6},{4,0},{6,2},{8,12},{10,14},{12,8},{14,10},{1,5},{3,7},... | collective-permute-start | bytes 393224 | tf_op jit(solution)/shard_map/ppermute | solution.py:25
  58.3 4.4 %collective-permute-start.11 = (bf16[64,4096]{1,0:T(8,128)(2,1)S(1)}, bf16[64,4096]{1,0:T(8,128)(2,1)S(1)}, u32[]{:S(2)}, u32[]{:S(2)}) collective-permute-start(bf16[64,4096]{1,0:T(8,128)(2,1)S(1)} %pad_maximum_fusion), channel_id=1, source_target_pairs={{0,16},{16,0},{1,17},{17,1},{2,18},{18,2},{3,19},{19,3},{4,20},{20... | collective-permute-start | bytes 1572872 | tf_op jit(solution)/shard_map/ppermute | solution.py:25
  62.7 0.4 shard_map.131
  63.1 0.7 collective-permute-done.8
  63.9 2.8 %collective-permute-start.9 = (bf16[8,4096]{1,0:T(8,128)(2,1)S(1)}, bf16[8,4096]{1,0:T(8,128)(2,1)S(1)}, u32[]{:S(2)}, u32[]{:S(2)}) collective-permute-start(bf16[8,4096]{1,0:T(8,128)(2,1)S(1)} %slice.52), channel_id=1, source_target_pairs={{0,8},{2,10},{4,12},{6,14},{8,0},{10,2},{12,4},{14,6},{1,9},{3,11}... | collective-permute-start | bytes 196616 | tf_op jit(solution)/shard_map/ppermute | solution.py:25
  66.7 2.2 %collective-permute-start.14 = (f32[8,2048]{1,0:T(8,128)S(1)}, f32[8,2048]{1,0:T(8,128)S(1)}, u32[]{:S(2)}, u32[]{:S(2)}) collective-permute-start(f32[8,2048]{1,0:T(8,128)S(1)} %add.46), channel_id=1, source_target_pairs={{0,64},{64,0},{128,192},{192,128},{256,320},{320,256},{384,448},{4... | collective-permute-start | bytes 196616 | tf_op jit(solution)/shard_map/ppermute | solution.py:25
  68.9 3.3 %collective-permute-done.11 = bf16[64,4096]{1,0:T(8,128)(2,1)S(1)} collective-permute-done((bf16[64,4096]{1,0:T(8,128)(2,1)S(1)}, bf16[64,4096]{1,0:T(8,128)(2,1)S(1)}, u32[]{:S(2)}, u32[]{:S(2)}) %collective-permute-start.11) | collective-permute-done | bytes 524320 | tf_op jit(solution)/shard_map/ppermute | solution.py:25
  72.3 5.7 %collective-permute-start.12 = (bf16[128,4096]{1,0:T(8,128)(2,1)S(1)}, bf16[128,4096]{1,0:T(8,128)(2,1)S(1)}, u32[]{:S(2)}, u32[]{:S(2)}) collective-permute-start(bf16[128,4096]{1,0:T(8,128)(2,1)S(1)} %constant_dynamic-update-slice_fusion.4.mine), channel_id=1, source_target_pairs={{0,1},{1,0},{2,3},{3,2},{4,5},{5,4},{6,7},{7,6},{8,9},{9,8},{10,11... | collective-permute-start | bytes 3145736 | tf_op jit(solution)/shard_map/ppermute | solution.py:25
  78.0 0.7 multiply_bitcast_fusion
  78.7 0.7 multiply_subtract_fusion
  79.4 0.8 %shard_map.130.grad = f32[320,128]{1,0:T(8,128)S(1)} custom-call(bf16[320,4096]{1,0:T(8,128)(2,1)S(1)} %copy-done, bf16[128,4096]{1,0:T(8,128)(2,1)S(1)} %constant_dynamic-update-slice_fusion.4.mine), custom_call_target="tpu_custom_call" | custom-call | flops 335544320 | bytes 16777216 | tf_op jit(solution)/shard_map/pallas_call | solution.py:209
  80.3 1.8 %shard_map.132 = (bf16[320,256]{1,0:T(8,128)(2,1)}, bf16[320,256]{1,0:T(8,128)(2,1)}) custom-call(bf16[320,4096]{1,0:T(8,128)(2,1)S(1)} %copy-done, bf16[128,4096]{1,0:T(8,128)(2,1)S(1)} %collective-permute-done.12.other, f32[320,128]{1,0:T(8,128)S(1)} %shard_map.130.grad, f32[320,256]{1,0:T(8,128)S(1)} %get-tuple-element.46.by_gate, ...), custom_call_target="tpu_custom_call" | custom-call | flops 335544320 | bytes 4194304 | tf_op jit(solution)/shard_map/pallas_call | solution.py:216
  (50 shorter events, 0.8 us)
Async XLA Ops:
  0.6 13.1 %copy-start.7 = (f32[1,8,32]{2,1,0:T(8,128)S(1)}, f32[1,8,32]{2,1,0:T(8,128)}, u32[]{:S(2)}) copy-start(f32[1,8,32]{2,1,0:T(8,128)} %param.16) | copy-start | bytes 3076
  0.6 13.2 %copy-start.4 = (s32[1,8,4096]{2,1,0:T(8,128)S(1)}, s32[1,8,4096]{2,1,0:T(8,128)}, u32[]{:S(2)}) copy-start(s32[1,8,4096]{2,1,0:T(8,128)} %param.15) | copy-start | bytes 393220
  0.7 15.2 %copy-start.6 = (bf16[8,4096]{1,0:T(8,128)(2,1)S(1)}, bf16[8,4096]{1,0:T(8,128)(2,1)}, u32[]{:S(2)}) copy-start(bf16[8,4096]{1,0:T(8,128)(2,1)} %param.12) | copy-start | bytes 196612
  4.9 15.8 %collective-permute-start = (bf16[128,4096]{1,0:T(8,128)(2,1)}, bf16[128,4096]{1,0:T(8,128)(2,1)S(1)}, u32[]{:S(2)}, u32[]{:S(2)}) collective-permute-start(bf16[128,4096]{1,0:T(8,128)(2,1)} %get-tuple-element.29), channel_id=1, source_target_pairs={{0,1},{1,0},{2,3},{3,2},{4,5},{5,4},{6,7},{7,6},{8,9},{9,8},{10,11... | collective-permute-start | bytes 3145736 | tf_op jit(solution)/shard_map/ppermute | solution.py:25
  13.9 6.9 %collective-permute-start.1 = (f32[8,2048]{1,0:T(8,128)S(1)}, f32[8,2048]{1,0:T(8,128)S(1)}, u32[]{:S(2)}, u32[]{:S(2)}) collective-permute-start(f32[8,2048]{1,0:T(8,128)S(1)} %get-tuple-element.53), channel_id=1, source_target_pairs={{0,64},{64,0},{128,192},{192,128},{256,320},{320,256},{384,448},{4... | collective-permute-start | bytes 196616 | tf_op jit(solution)/shard_map/ppermute | solution.py:25
  15.9 12.5 %collective-permute-start.4 = (bf16[8,4096]{1,0:T(8,128)(2,1)S(1)}, bf16[8,4096]{1,0:T(8,128)(2,1)S(1)}, u32[]{:S(2)}, u32[]{:S(2)}) collective-permute-start(bf16[8,4096]{1,0:T(8,128)(2,1)S(1)} %copy-done.6), channel_id=1, source_target_pairs={{0,8},{2,10},{4,12},{6,14},{8,0},{10,2},{12,4},{14,6},{1,9},{3,11}... | collective-permute-start | bytes 196616 | tf_op jit(solution)/shard_map/ppermute | solution.py:25
  20.9 10.0 %collective-permute-start.2 = (f32[8,2048]{1,0:T(8,128)S(1)}, f32[8,2048]{1,0:T(8,128)S(1)}, u32[]{:S(2)}, u32[]{:S(2)}) collective-permute-start(f32[8,2048]{1,0:T(8,128)S(1)} %add.39), channel_id=1, source_target_pairs={{0,32},{32,0},{1,33},{33,1},{2,34},{34,2},{3,35},{35,3},{4,36},{36... | collective-permute-start | bytes 196616 | tf_op jit(solution)/shard_map/ppermute | solution.py:25
  24.0 16.0 %collective-permute-start.3 = (bf16[64,4096]{1,0:T(8,128)(2,1)S(1)}, bf16[64,4096]{1,0:T(8,128)(2,1)S(1)}, u32[]{:S(2)}, u32[]{:S(2)}) collective-permute-start(bf16[64,4096]{1,0:T(8,128)(2,1)S(1)} %get-tuple-element.34), channel_id=1, source_target_pairs={{0,16},{16,0},{1,17},{17,1},{2,18},{18,2},{3,19},{19,3},{4,20},{20... | collective-permute-start | bytes 1572872 | tf_op jit(solution)/shard_map/ppermute | solution.py:25
  28.4 14.2 %collective-permute-start.6 = (bf16[16,4096]{1,0:T(8,128)(2,1)S(1)}, bf16[16,4096]{1,0:T(8,128)(2,1)S(1)}, u32[]{:S(2)}, u32[]{:S(2)}) collective-permute-start(bf16[16,4096]{1,0:T(8,128)(2,1)S(1)} %constant_dynamic-update-slice_fusion), channel_id=1, source_target_pairs={{0,4},{2,6},{4,0},{6,2},{8,12},{10,14},{12,8},{14,10},{1,5},{3,7},... | collective-permute-start | bytes 393224 | tf_op jit(solution)/shard_map/ppermute | solution.py:25
  30.9 14.8 %collective-permute-start.7 = (f32[8,2048]{1,0:T(8,128)S(1)}, f32[8,2048]{1,0:T(8,128)S(1)}, u32[]{:S(2)}, u32[]{:S(2)}) collective-permute-start(f32[8,2048]{1,0:T(8,128)S(1)} %add.40), channel_id=1, source_target_pairs={{0,128},{64,192},{128,0},{192,64},{256,384},{320,448},{384,256},{4... | collective-permute-start | bytes 196616 | tf_op jit(solution)/shard_map/ppermute | solution.py:25
  40.1 22.6 %copy-start.1 = (bf16[320,256]{1,0:T(8,128)(2,1)S(1)}, bf16[320,256]{1,0:T(8,128)(2,1)}, u32[]{:S(2)}) copy-start(bf16[320,256]{1,0:T(8,128)(2,1)} %gate.2) | copy-start | bytes 491524
  40.1 22.6 %copy-start.2 = (bf16[320,256]{1,0:T(8,128)(2,1)S(1)}, bf16[320,256]{1,0:T(8,128)(2,1)}, u32[]{:S(2)}) copy-start(bf16[320,256]{1,0:T(8,128)(2,1)} %up.2) | copy-start | bytes 491524
  40.2 15.2 %collective-permute-start.5 = (bf16[32,4096]{1,0:T(8,128)(2,1)S(1)}, bf16[32,4096]{1,0:T(8,128)(2,1)S(1)}, u32[]{:S(2)}, u32[]{:S(2)}) collective-permute-start(bf16[32,4096]{1,0:T(8,128)(2,1)S(1)} %slice.50), channel_id=1, source_target_pairs={{0,2},{2,0},{4,6},{6,4},{8,10},{10,8},{12,14},{14,12},{1,3},{3,1},... | collective-permute-start | bytes 786440 | tf_op jit(solution)/shard_map/ppermute | solution.py:25
  42.7 15.6 %collective-permute-start.10 = (bf16[32,4096]{1,0:T(8,128)(2,1)S(1)}, bf16[32,4096]{1,0:T(8,128)(2,1)S(1)}, u32[]{:S(2)}, u32[]{:S(2)}) collective-permute-start(bf16[32,4096]{1,0:T(8,128)(2,1)S(1)} %constant_dynamic-update-slice_fusion.2), channel_id=1, source_target_pairs={{0,2},{2,0},{4,6},{6,4},{8,10},{10,8},{12,14},{14,12},{1,3},{3,1},... | collective-permute-start | bytes 786440 | tf_op jit(solution)/shard_map/ppermute | solution.py:25
  45.7 21.0 %collective-permute-start.13 = (f32[8,2048]{1,0:T(8,128)S(1)}, f32[8,2048]{1,0:T(8,128)S(1)}, u32[]{:S(2)}, u32[]{:S(2)}) collective-permute-start(f32[8,2048]{1,0:T(8,128)S(1)} %add.43), channel_id=1, source_target_pairs={{0,256},{64,320},{128,384},{192,448},{256,0},{320,64},{384,128},{4... | collective-permute-start | bytes 196616 | tf_op jit(solution)/shard_map/ppermute | solution.py:25
  55.5 23.2 %copy-start.3 = (f32[8,4096]{1,0:T(8,128)S(1)}, f32[8,4096]{1,0:T(8,128)}, u32[]{:S(2)}) copy-start(f32[8,4096]{1,0:T(8,128)} %param.13) | copy-start | bytes 393220
  55.5 23.2 %copy-start.5 = (f32[2,8,4096]{2,1,0:T(8,128)S(1)}, f32[2,8,4096]{2,1,0:T(8,128)}, u32[]{:S(2)}) copy-start(f32[2,8,4096]{2,1,0:T(8,128)} %param.14) | copy-start | bytes 786436
  55.5 23.9 %copy-start = (bf16[320,4096]{1,0:T(8,128)(2,1)S(1)}, bf16[320,4096]{1,0:T(8,128)(2,1)}, u32[]{:S(2)}) copy-start(bf16[320,4096]{1,0:T(8,128)(2,1)} %cot.5) | copy-start | bytes 7864324
  55.5 8.3 %collective-permute-start.8 = (bf16[16,4096]{1,0:T(8,128)(2,1)S(1)}, bf16[16,4096]{1,0:T(8,128)(2,1)S(1)}, u32[]{:S(2)}, u32[]{:S(2)}) collective-permute-start(bf16[16,4096]{1,0:T(8,128)(2,1)S(1)} %slice.51), channel_id=1, source_target_pairs={{0,4},{2,6},{4,0},{6,2},{8,12},{10,14},{12,8},{14,10},{1,5},{3,7},... | collective-permute-start | bytes 393224 | tf_op jit(solution)/shard_map/ppermute | solution.py:25
  58.3 13.9 %collective-permute-start.11 = (bf16[64,4096]{1,0:T(8,128)(2,1)S(1)}, bf16[64,4096]{1,0:T(8,128)(2,1)S(1)}, u32[]{:S(2)}, u32[]{:S(2)}) collective-permute-start(bf16[64,4096]{1,0:T(8,128)(2,1)S(1)} %pad_maximum_fusion), channel_id=1, source_target_pairs={{0,16},{16,0},{1,17},{17,1},{2,18},{18,2},{3,19},{19,3},{4,20},{20... | collective-permute-start | bytes 1572872 | tf_op jit(solution)/shard_map/ppermute | solution.py:25
  63.9 14.1 %collective-permute-start.9 = (bf16[8,4096]{1,0:T(8,128)(2,1)S(1)}, bf16[8,4096]{1,0:T(8,128)(2,1)S(1)}, u32[]{:S(2)}, u32[]{:S(2)}) collective-permute-start(bf16[8,4096]{1,0:T(8,128)(2,1)S(1)} %slice.52), channel_id=1, source_target_pairs={{0,8},{2,10},{4,12},{6,14},{8,0},{10,2},{12,4},{14,6},{1,9},{3,11}... | collective-permute-start | bytes 196616 | tf_op jit(solution)/shard_map/ppermute | solution.py:25
  66.7 12.0 %collective-permute-start.14 = (f32[8,2048]{1,0:T(8,128)S(1)}, f32[8,2048]{1,0:T(8,128)S(1)}, u32[]{:S(2)}, u32[]{:S(2)}) collective-permute-start(f32[8,2048]{1,0:T(8,128)S(1)} %add.46), channel_id=1, source_target_pairs={{0,64},{64,0},{128,192},{192,128},{256,320},{320,256},{384,448},{4... | collective-permute-start | bytes 196616 | tf_op jit(solution)/shard_map/ppermute | solution.py:25
  72.3 8.0 %collective-permute-start.12 = (bf16[128,4096]{1,0:T(8,128)(2,1)S(1)}, bf16[128,4096]{1,0:T(8,128)(2,1)S(1)}, u32[]{:S(2)}, u32[]{:S(2)}) collective-permute-start(bf16[128,4096]{1,0:T(8,128)(2,1)S(1)} %constant_dynamic-update-slice_fusion.4.mine), channel_id=1, source_target_pairs={{0,1},{1,0},{2,3},{3,2},{4,5},{5,4},{6,7},{7,6},{8,9},{9,8},{10,11... | collective-permute-start | bytes 3145736 | tf_op jit(solution)/shard_map/ppermute | solution.py:25
